TPU v7x, 128 devices: a whole 4x4x4 slice. The times are simulated.
128 devices in a mesh: chan: 32 (over z_lo, x, y), seg: 4 (over z_hi, core).
Axes of the slice: x: 4, y: 4, z: 4 (z_hi: 2, z_lo: 2; z = z_hi * 2 + z_lo), core: 2. Of those that a mesh axis runs over, the one named last changes fastest.
Arguments:
- traces: bfloat16 [1024, 16, 8192], P('chan', 'seg'), may hold values from -6 to 6
- alive: int32 [1024], P('chan'), may hold values 0 or 1
- pair_chan: int32 [4096, 2], P('chan'), may hold values from 0 to 1023, as said below
- lag_window: int32 [4096], P(('chan', 'seg')), may hold values from 4 to 256
Outputs:
- correlation: float32 [4096, 512], P(('chan', 'seg'))
Inputs may be any that keep to these rules, and one draw needn't show every extreme that they name: `pair_chan`: row p holds channels i < j with j - i at most 125, and i lies in the block of 32 channels numbered p // 128.
All inputs are finite; a program needn't handle non-finite values. No bound on the sum of `alive` on one device may be relied on, other than what follows from the above.
Results may differ from a plain program's by a relative error of at most 0.014.
Values may be sent and summed in bfloat16 or wider, within the bound.
A program may use at most 384 MiB of HBM per device.

v0:
```python
import math

import jax
import jax.numpy as jnp
from jax import lax
from jax.sharding import PartitionSpec as P

FREQ = 4096
SAMP = 8192
BAND = 64
LAGS = 512
REACH = 125


eps_whiten = 1e-06


def shifted(block, axis, distance):
    devices = range(lax.axis_size(axis))
    route = [(i - distance, i) for i in devices if i - distance in devices]
    return lax.ppermute(block, axis, route)


def dft_table(first_bin, width):
    time_index = jnp.arange(SAMP, dtype=jnp.int32)[:, None]
    bin_index = first_bin + jnp.arange(width, dtype=jnp.int32)[None, :]
    phase = time_index * bin_index % SAMP
    angle = phase.astype(jnp.float32) * (2.0 * math.pi / SAMP)
    return jnp.concatenate([jnp.cos(angle), -jnp.sin(angle)], axis=1).astype(jnp.bfloat16)


def band_scale(real_part, imag_part):
    magnitude = jnp.sqrt(real_part * real_part + imag_part * imag_part)
    level = magnitude.reshape(magnitude.shape[0], -1, BAND).mean(axis=2)
    return jnp.repeat(1.0 / (level + eps_whiten), BAND, axis=1)


def lag_table():
    freq_index = jnp.arange(FREQ, dtype=jnp.int32)[:, None]
    lag_shift = (jnp.arange(LAGS, dtype=jnp.int32) - LAGS // 2) % SAMP
    phase = freq_index * lag_shift[None, :] % SAMP
    angle = phase.astype(jnp.float32) * (2.0 * math.pi / SAMP)
    return jnp.concatenate([jnp.cos(angle), -jnp.sin(angle)], axis=0)


def whiten_rows(trace_rows, live_rows):
    block_bins = min(FREQ, 512)
    real_pieces = []
    imag_pieces = []
    for first_bin in range(0, FREQ, block_bins):
        table = dft_table(first_bin, block_bins)
        spectrum = jnp.dot(trace_rows, table, preferred_element_type=jnp.float32)
        real_part = spectrum[:, :block_bins]
        imag_part = spectrum[:, block_bins:]
        scale = band_scale(real_part, imag_part) * live_rows[:, None]
        real_pieces.append(real_part * scale)
        imag_pieces.append(imag_part * scale)
    return jnp.concatenate(real_pieces + imag_pieces, axis=1).astype(jnp.bfloat16)


def body(traces, alive, pair_chan, lag_window):
    chan_count, seg_count, samples = traces.shape
    live = alive.astype(jnp.float32)
    ahead_blocks = (REACH + chan_count - 1) // chan_count
    own_spectra = whiten_rows(
        traces.reshape(chan_count * seg_count, samples), jnp.repeat(live, seg_count)
    )
    own_spectra = own_spectra.reshape(chan_count, seg_count, 2 * FREQ)
    ahead_list = []
    for block_step in range(1, ahead_blocks + 1):
        ahead_list.append(shifted(own_spectra, "chan", -block_step))
    ahead_spectra = jnp.concatenate(ahead_list, axis=0)
    extended = jnp.concatenate([own_spectra, ahead_spectra], axis=0)
    local_pairs = pair_chan - lax.axis_index("chan") * chan_count
    seg_devices = lax.axis_size("seg")
    factor = 1.0 / math.sqrt(seg_count * seg_devices * FREQ)
    lags_matrix = lag_table()
    first_side = jnp.take(extended, local_pairs[:, 0], axis=0).astype(jnp.float32)
    second_side = jnp.take(extended, local_pairs[:, 1], axis=0).astype(jnp.float32)
    first_real = first_side[..., :FREQ]
    first_imag = first_side[..., FREQ:]
    second_real = second_side[..., :FREQ]
    second_imag = second_side[..., FREQ:]
    cross_real = jnp.sum(first_real * second_real + first_imag * second_imag, axis=1) * factor
    cross_imag = jnp.sum(first_imag * second_real - first_real * second_imag, axis=1) * factor
    lagged = lax.psum_scatter(
        jnp.dot(
            jnp.concatenate([cross_real, cross_imag], axis=1),
            lags_matrix,
            precision=lax.Precision.HIGHEST,
            preferred_element_type=jnp.float32,
        ).astype(jnp.bfloat16),
        "seg",
        scatter_dimension=0,
        tiled=True,
    ).astype(jnp.float32)
    lag_value = jnp.abs(jnp.arange(LAGS, dtype=jnp.int32) - LAGS // 2)
    keep = lag_value[None, :] <= lag_window[:, None]
    return jnp.where(keep, lagged, jnp.zeros_like(lagged))


def solution(mesh):
    in_specs = (P("chan", "seg", None), P("chan"), P("chan", None), P(("chan", "seg")))
    out_specs = P(("chan", "seg"), None)
    return jax.shard_map(body, mesh=mesh, in_specs=in_specs, out_specs=out_specs, check_vma=False)
```

profile of v0, /device:TPU:1, one launch (start us, length us, event | category | flops | bytes accessed | tf_op | source)
XLA Modules:
  0.0 1136.3 jit_solution(9686623461352656432)
XLA Ops:
  6.5 68.8 %negate_convert_fusion.7 = (bf16[8192,512]{1,0:T(8,128)(2,1)}, bf16[8192,512]{1,0:T(8,128)(2,1)}) fusion(), kind=kLoop, calls=%fused_computation.114 | loop fusion | flops 71303168 | bytes 16777216 | tf_op jit(solution)/shard_map/convert.47
  76.5 2.0 reshape.144
  78.6 67.4 %cosine_convert_fusion.6 = (bf16[8192,512]{1,0:T(8,128)(2,1)S(1)}, bf16[8192,512]{1,0:T(8,128)(2,1)S(1)}) fusion(s32[512]{0:T(512)S(1)} %iota_add_fusion.6), kind=kLoop, calls=%fused_computation.111 | loop fusion | flops 71303168 | bytes 16779264 | tf_op jit(solution)/shard_map/convert.44
  146.0 2.3 fusion.112
  148.8 7.1 fusion.115
  156.8 1.8 copy.5
  158.6 1.0 bitcast_reduce_fusion.7
  160.3 1.8 copy.6
  162.9 1.9 multiply_convert_fusion.6
  166.5 68.6 %cosine_convert_fusion.5 = (bf16[8192,512]{1,0:T(8,128)(2,1)S(1)}, bf16[8192,512]{1,0:T(8,128)(2,1)S(1)}) fusion(s32[512]{0:T(512)} %iota_add_fusion.5), kind=kLoop, calls=%fused_computation.107 | loop fusion | flops 71303168 | bytes 16779264 | tf_op jit(solution)/shard_map/convert.42
  235.1 2.3 fusion.109
  237.9 67.7 %cosine_convert_fusion.4 = (bf16[8192,512]{1,0:T(8,128)(2,1)S(1)}, bf16[8192,512]{1,0:T(8,128)(2,1)S(1)}) fusion(s32[512]{0:T(512)S(1)} %iota_add_fusion.4), kind=kLoop, calls=%fused_computation.103 | loop fusion | flops 71303168 | bytes 16779264 | tf_op jit(solution)/shard_map/convert.40
  305.6 2.3 fusion.106
  309.1 67.4 %cosine_convert_fusion.3 = (bf16[8192,512]{1,0:T(8,128)(2,1)S(1)}, bf16[8192,512]{1,0:T(8,128)(2,1)S(1)}) fusion(s32[512]{0:T(512)S(1)} %iota_add_fusion.3), kind=kLoop, calls=%fused_computation.99 | loop fusion | flops 71303168 | bytes 16779264 | tf_op jit(solution)/shard_map/convert.38
  376.5 3.9 fusion.103
  381.5 67.9 %cosine_convert_fusion.2 = (bf16[8192,512]{1,0:T(8,128)(2,1)S(1)}, bf16[8192,512]{1,0:T(8,128)(2,1)S(1)}) fusion(s32[512]{0:T(512)S(1)} %iota_add_fusion.2), kind=kLoop, calls=%fused_computation.95 | loop fusion | flops 71303168 | bytes 16779264 | tf_op jit(solution)/shard_map/convert.36
  449.4 3.9 fusion.100
  454.5 67.6 %cosine_convert_fusion.1 = (bf16[8192,512]{1,0:T(8,128)(2,1)S(1)}, bf16[8192,512]{1,0:T(8,128)(2,1)S(1)}) fusion(s32[512]{0:T(512)S(1)} %iota_add_fusion.1), kind=kLoop, calls=%fused_computation.91 | loop fusion | flops 71303168 | bytes 16779264 | tf_op jit(solution)/shard_map/convert.34
  522.1 3.9 fusion.97
  527.1 67.4 %cosine_convert_fusion = (bf16[8192,512]{1,0:T(8,128)(2,1)S(1)}, bf16[8192,512]{1,0:T(8,128)(2,1)S(1)}) fusion(s32[512]{0:T(512)S(1)} %copy-done.3), kind=kLoop, calls=%fused_computation.87 | loop fusion | flops 71303168 | bytes 16779264 | tf_op jit(solution)/shard_map/convert.32
  594.6 3.9 fusion.94
  599.3 1.8 copy.19
  601.1 1.0 bitcast_reduce_fusion
  602.8 1.8 copy.20
  604.6 2.8 multiply_convert_fusion
  608.3 0.9 concatenate.85
  609.2 0.9 concatenate.87
  610.2 0.9 concatenate.89
  611.1 0.9 concatenate.91
  632.5 1.3 collective-permute-start
  633.8 1.3 collective-permute-start.1
  635.1 1.3 collective-permute-start.2
  636.4 1.5 collective-permute-start.3
  638.0 34.6 %fusion.93 = (f32[4096,512]{1,0:T(8,128)}, f32[4096,512]{1,0:T(8,128)}) fusion(s32[512]{0:T(512)S(1)} %add_select_fusion.9), kind=kLoop, calls=%fused_computation.143 | loop fusion | flops 31457280 | bytes 16779264 | tf_op jit(solution)/shard_map/cos | solution.py:43
  672.7 54.1 %collective-permute-done = bf16[32,4,8192]{2,1,0:T(4,128)(2,1)} collective-permute-done((bf16[32,4,8192]{2,1,0:T(4,128)(2,1)}, bf16[32,4,8192]{2,1,0:T(4,128)(2,1)}, u32[]{:S(2)}, u32[]{:S(2)}) %collective-permute-start) | collective-permute-done | bytes 2097184 | tf_op jit(solution)/shard_map/ppermute | solution.py:21
  726.8 4.2 constant_dynamic-update-slice_fusion.19
  730.9 4.2 constant_dynamic-update-slice_fusion.18
  735.1 4.2 constant_dynamic-update-slice_fusion.17
  739.3 159.0 %collective-permute-done.3 = bf16[32,4,8192]{2,1,0:T(4,128)(2,1)S(1)} collective-permute-done((bf16[32,4,8192]{2,1,0:T(4,128)(2,1)}, bf16[32,4,8192]{2,1,0:T(4,128)(2,1)S(1)}, u32[]{:S(2)}, u32[]{:S(2)}) %collective-permute-start.3) | collective-permute-done | bytes 2097184 | tf_op jit(solution)/shard_map/ppermute | solution.py:21
  898.3 2.2 constant_dynamic-update-slice_fusion.16
  900.5 14.6 %gather_fusion = bf16[128,4,8192]{2,1,0:T(4,128)(2,1)} fusion(bf16[160,4,8192]{2,1,0:T(4,128)(2,1)} %constant_dynamic-update-slice_fusion.16, s32[1024]{0:T(1024)S(1)} %get-tuple-element.93), kind=kCustom, calls=%fused_computation.clone | custom fusion | bytes 16777728 | tf_op jit(solution)/shard_map/jit(_take)/gather | solution.py:78
  915.2 14.7 %gather_fusion.1 = bf16[128,4,8192]{2,1,0:T(4,128)(2,1)} fusion(bf16[160,4,8192]{2,1,0:T(4,128)(2,1)} %constant_dynamic-update-slice_fusion.16, s32[1024]{0:T(1024)S(1)} %get-tuple-element.92), kind=kCustom, calls=%fused_computation.1.clone | custom fusion | bytes 16777728 | tf_op jit(solution)/shard_map/jit(_take)/gather | solution.py:79
  929.9 6.1 select_convert_fusion.1
  936.0 6.2 select_convert_fusion
  942.2 21.3 %add_reduce_fusion = (f32[128,4096]{1,0:T(8,128)S(1)}, f32[128,4096]{1,0:T(8,128)S(1)}) fusion(f32[128,4,8192]{2,1,0:T(4,128)} %select_convert_fusion, f32[128,4,8192]{2,1,0:T(4,128)S(1)} %select_convert_fusion.1), kind=kLoop, calls=%fused_computation.138 | loop fusion | flops 15728640 | bytes 37748736 | tf_op jit(solution)/shard_map/reduce_sum | solution.py:84
  963.9 12.2 %fusion.118 = bf16[128,512]{1,0:T(8,128)(2,1)} fusion(f32[4096,512]{1,0:T(8,128)} %get-tuple-element.75, f32[4096,512]{1,0:T(8,128)} %get-tuple-element.74, f32[128,4096]{1,0:T(8,128)S(1)} %broadcast_multiply_fusion, f32[128,4096]{1,0:T(8,128)S(1)} %broadcast_multiply_fusion.1), kind=kOutput, calls=%fused_computation.152 | convolution fusion | flops 6447759360 | bytes 21102592 | tf_op jit(solution)/shard_map/dot_general | solution.py:87
  976.1 151.4 %reduce-scatter.2.cloned.1.call-done = bf16[32,512]{1,0:T(8,128)(2,1)} async-done(((bf16[128,512]{1,0:T(8,128)(2,1)}), bf16[32,512]{1,0:T(8,128)(2,1)}) %reduce-scatter.2.cloned.1.call-update) | async-done | bytes 32784 | tf_op jit(solution)/shard_map/reduce_scatter | solution.py:86
  1127.5 1.5 convert_select_fusion
  (107 shorter events, 33.9 us)
Async XLA Ops:
  6.5 70.0 %copy-start.1 = (bf16[32,4,8192]{2,1,0:T(4,128)(2,1)S(1)}, bf16[32,4,8192]{2,1,0:T(4,128)(2,1)}, u32[]{:S(2)}) copy-start(bf16[32,4,8192]{2,1,0:T(4,128)(2,1)} %param.6) | copy-start | bytes 6291460
  6.5 1121.0 %reduce-scatter.2.cloned.1.call-start = ((), (), s32[]{:S(2)}) async-start(), calls=%async_computation.1 | async-start | bytes 163840 | tf_op jit(solution)/shard_map/reduce_scatter | solution.py:86
  78.6 67.4 %copy-start.2 = (bf16[128,8192]{1,0:T(8,128)(2,1)S(1)}, bf16[128,8192]{1,0:T(8,128)(2,1)}, u32[]{:S(2)}) copy-start(bf16[128,8192]{1,0:T(8,128)(2,1)} %reshape.144) | copy-start | bytes 6291460
  148.8 13.3 %copy-start.7 = (s32[32]{0:T(128)S(1)}, s32[32]{0:T(128)}, u32[]{:S(2)}) copy-start(s32[32]{0:T(128)} %param.7) | copy-start | bytes 388
  522.0 5.1 copy-start.3
  594.5 10.0 copy-start.4
  598.5 39.5 %copy-start.5 = (s32[128,2]{0,1:T(2,128)S(1)}, s32[128,2]{0,1:T(2,128)}, u32[]{:S(2)}) copy-start(s32[128,2]{0,1:T(2,128)} %param.8) | copy-start | bytes 3076
  632.5 94.2 %collective-permute-start = (bf16[32,4,8192]{2,1,0:T(4,128)(2,1)}, bf16[32,4,8192]{2,1,0:T(4,128)(2,1)}, u32[]{:S(2)}, u32[]{:S(2)}) collective-permute-start(bf16[32,4,8192]{2,1,0:T(4,128)(2,1)} %get-tuple-element.28), channel_id=1, source_target_pairs={{4,0},{8,4},{12,8},{16,12},{20,16},{24,20},{28,24},{32,28},{36,32}... | collective-permute-start | bytes 6291464 | tf_op jit(solution)/shard_map/ppermute | solution.py:21
  633.8 97.1 %collective-permute-start.1 = (bf16[32,4,8192]{2,1,0:T(4,128)(2,1)}, bf16[32,4,8192]{2,1,0:T(4,128)(2,1)}, u32[]{:S(2)}, u32[]{:S(2)}) collective-permute-start(bf16[32,4,8192]{2,1,0:T(4,128)(2,1)} %get-tuple-element.28), channel_id=1, source_target_pairs={{8,0},{12,4},{16,8},{20,12},{24,16},{28,20},{32,24},{36,28},{40,32... | collective-permute-start | bytes 6291464 | tf_op jit(solution)/shard_map/ppermute | solution.py:21
  635.1 99.9 %collective-permute-start.2 = (bf16[32,4,8192]{2,1,0:T(4,128)(2,1)}, bf16[32,4,8192]{2,1,0:T(4,128)(2,1)}, u32[]{:S(2)}, u32[]{:S(2)}) collective-permute-start(bf16[32,4,8192]{2,1,0:T(4,128)(2,1)} %get-tuple-element.28), channel_id=1, source_target_pairs={{12,0},{16,4},{20,8},{24,12},{28,16},{32,20},{36,24},{40,28},{44,3... | collective-permute-start | bytes 6291464 | tf_op jit(solution)/shard_map/ppermute | solution.py:21
  636.4 261.9 %collective-permute-start.3 = (bf16[32,4,8192]{2,1,0:T(4,128)(2,1)}, bf16[32,4,8192]{2,1,0:T(4,128)(2,1)S(1)}, u32[]{:S(2)}, u32[]{:S(2)}) collective-permute-start(bf16[32,4,8192]{2,1,0:T(4,128)(2,1)} %get-tuple-element.28), channel_id=1, source_target_pairs={{16,0},{20,4},{24,8},{28,12},{32,16},{36,20},{40,24},{44,28},{48,3... | collective-permute-start | bytes 6291464 | tf_op jit(solution)/shard_map/ppermute | solution.py:21
  929.9 6.1 copy-start
  963.9 163.7 %copy-start.6 = (s32[32]{0:T(128)S(1)}, s32[32]{0:T(128)}, u32[]{:S(2)}) copy-start(s32[32]{0:T(128)} %param.9) | copy-start | bytes 388
Sparse Core Ops, SparseCore 0:
  976.2 151.2 reduce-scatter.1
where the time goes:
time: 1150 us; the launch traced here: 1140 us
  other arithmetic  623 us (54%)
  waiting for transfers between devices  365 us (32%)
  local copies, waits for them, and re-layouts  87 us (8%)
  matrix products  42 us (4%)
  between operations  14.4 us (1%)
    another operation x10, other arithmetic  547 us
    ppermute x4, waiting for transfers between devices, shifted(): return lax.ppermute(block, axis, route)  213 us
    reduce_scatter x1, waiting for transfers between devices, body(): lax.psum_scatter(jnp.dot(jnp.concatenate([cross_real, cross_imag], axis=1...  151 us
    cos x1, other arithmetic, lag_table(): return jnp.concatenate([jnp.cos(angle), -jnp.sin(angle)], axis=0)  34.6 us
    dot_general x8, matrix products, whiten_rows(): spectrum = jnp.dot(trace_rows, table, preferred_element_type=jnp.float32)  29.9 us
    unnamed x34, local copies, waits for them, and re-layouts  24.5 us
  transfers between devices with their start and end apart: 5, of which 3 were waited for; matrix products, arithmetic and copies ran while one was open for 4% of the time, Pallas kernels for 0%

commit v1 on v0

v1 whole, which is shorter than its diff:
```python
import functools
import math

import jax
import jax.numpy as jnp
import numpy as np
from jax import lax
from jax.experimental import pallas as pl
from jax.experimental.pallas import tpu as pltpu
from jax.sharding import PartitionSpec as P

FREQ = 4096
SAMP = 8192
BAND = 64
LAGS = 512
UNITS = 32
ROW = 4
CH = 32
SEG = 4
EPS = 1e-06


def unit_bins():
    u = np.arange(UNITS)[:, None]
    lane = np.arange(128)[None, :]
    low = np.where(lane < 64, u, np.where(u == 0, 32, 64 - u))
    return low + 64 * (lane % 64)


def second_table():
    bins = unit_bins()[:, None, :]
    t2 = np.arange(128)[None, :, None]
    angle = 2.0 * np.pi * ((t2 * bins) % SAMP) / SAMP
    c, s = np.cos(angle), np.sin(angle)
    first = np.arange(128)[None, None, :] < 64
    unit0 = np.arange(UNITS)[:, None, None] == 0
    sign = np.where(first, 1.0, -1.0)
    rr = np.where(unit0, np.where(first, c, 0.0), c)
    ri = np.where(unit0, np.where(first, -s, 0.0), -s)
    ir = np.where(unit0, np.where(first, 0.0, c), sign * s)
    ii = np.where(unit0, np.where(first, 0.0, -s), sign * c)
    top = np.concatenate([rr, ri], axis=2)
    bottom = np.concatenate([ir, ii], axis=2)
    return np.concatenate([top, bottom], axis=1).astype(jnp.bfloat16)


def lag_table():
    bins = unit_bins()[:, :, None].astype(np.int64)
    tau = np.arange(LAGS)[None, None, :] - LAGS // 2
    angle = 2.0 * np.pi * ((bins * tau) % SAMP) / SAMP
    return (np.concatenate([np.cos(angle), -np.sin(angle)], axis=1) / 256.0).astype(jnp.bfloat16)


def real_dft(values):
    n = len(values)
    if n == 1:
        return [values[0]], [None]
    if n == 2:
        return [values[0] + values[1], values[0] - values[1]], [None, None]
    er, ei = real_dft(values[0::2])
    odr, odi = real_dft(values[1::2])
    half, quarter = n // 2, n // 4
    re, im = [None] * (half + 1), [None] * (half + 1)
    re[0], re[half] = er[0] + odr[0], er[0] - odr[0]
    re[quarter], im[quarter] = er[quarter], -odr[quarter]
    for k in range(1, quarter):
        c, s = math.cos(2 * math.pi * k / n), math.sin(2 * math.pi * k / n)
        if 8 * k == n:
            pr, pi = (odr[k] + odi[k]) * c, (odi[k] - odr[k]) * c
        else:
            pr, pi = odr[k] * c + odi[k] * s, odi[k] * c - odr[k] * s
        re[k], im[k] = er[k] + pr, ei[k] + pi
        re[half - k], im[half - k] = er[k] - pr, pi - ei[k]
    return re, im


def whiten_kernel(x_ref, live_ref, table_hbm, out_ref, mid, spec, level, table, sem):
    fetch = pltpu.make_async_copy(table_hbm, table, sem)
    fetch.start()

    def first_stage(block, carry):
        start = pl.multiple_of(block * 16, 16)
        for part in range(2):
            values = [
                x_ref[pl.ds(start, 16), pl.ds(128 * t, 128)].astype(jnp.float32)[8 * part : 8 * part + 8]
                for t in range(64)
            ]
            re, im = real_dft(values)
            rows = pl.ds(pl.multiple_of(start + 8 * part, 8), 8)
            mid[0, rows, 0:128] = re[0]
            mid[0, rows, 128:256] = re[32]
            for k in range(1, 32):
                mid[k, rows, 0:128] = re[k]
                mid[k, rows, 128:256] = im[k]
        return carry

    lax.fori_loop(0, 8, first_stage, 0)
    fetch.wait()
    level[...] = jnp.zeros_like(level)

    def second_stage(u, carry):
        got = jnp.dot(mid[u].astype(jnp.bfloat16), table[u], preferred_element_type=jnp.float32)
        re, im = got[:, :128], got[:, 128:]
        spec[u, 0] = re
        spec[u, 1] = im
        level[...] += jnp.sqrt(re * re + im * im)
        return carry

    lax.fori_loop(0, UNITS, second_stage, 0, unroll=4)
    total = level[...]
    level[...] = 1.0 / ((total + pltpu.roll(total, 64, 1)) * (1.0 / BAND) + EPS)

    def third_stage(u, carry):
        for s in range(SEG):
            scale = level[pl.ds(s, CH, stride=SEG), :] * live_ref[...]
            for half in range(2):
                cols = pl.ds(128 * half, 128)
                got = spec[u, half, pl.ds(s, CH, stride=SEG), :] * scale
                out_ref[u, s, :, cols] = got.astype(jnp.bfloat16)
        return carry

    lax.fori_loop(0, UNITS, third_stage, 0, unroll=2)


def whiten(rows, live, table):
    return pl.pallas_call(
        whiten_kernel,
        out_shape=jax.ShapeDtypeStruct((UNITS, SEG, CH, 256), jnp.bfloat16),
        in_specs=[
            pl.BlockSpec(memory_space=pltpu.VMEM),
            pl.BlockSpec(memory_space=pltpu.VMEM),
            pl.BlockSpec(memory_space=pl.ANY),
        ],
        out_specs=pl.BlockSpec(memory_space=pltpu.VMEM),
        scratch_shapes=[
            pltpu.VMEM((UNITS, 128, 256), jnp.float32),
            pltpu.VMEM((UNITS, 2, 128, 128), jnp.float32),
            pltpu.VMEM((128, 128), jnp.float32),
            pltpu.VMEM((UNITS, 256, 256), jnp.bfloat16),
            pltpu.SemaphoreType.DMA,
        ],
        compiler_params=pltpu.CompilerParams(vmem_limit_bytes=48 * 2**20),
    )(rows, live, table)


def pair_kernel(place, idx_ref, g_ref, h_ref, lag_ref, out_ref, first_pick, second_pick):
    unit = pl.program_id(0)
    late = unit // 4

    @pl.when(unit % 4 == 0)
    def _():
        lanes = lax.broadcasted_iota(jnp.int32, (512, 128), 1)
        i = idx_ref[0, :, 0:1]
        j = idx_ref[0, :, 1:2]
        first_pick[...] = jnp.where(lanes == i, 1.0, 0.0).astype(jnp.bfloat16)
        second_pick[:, 0:128] = jnp.where(lanes == j, 1.0, 0.0).astype(jnp.bfloat16)
        second_pick[:, 128:256] = jnp.where(lanes + 128 == j, 1.0, 0.0).astype(jnp.bfloat16)
        out_ref[...] = jnp.zeros_like(out_ref)

    def side(ref, s):
        return jnp.concatenate([ref[b, 0, s] for b in range(ROW)], axis=0)

    def work(near, far):
        cross_re = cross_im = None
        for s in range(SEG):
            own, other = side(near, s), side(far, s)
            a = jnp.dot(first_pick[...], own, preferred_element_type=jnp.float32)
            b = jnp.dot(second_pick[...], jnp.concatenate([own, other], axis=0), preferred_element_type=jnp.float32)
            ar, ai, br, bi = a[:, :128], a[:, 128:], b[:, :128], b[:, 128:]
            re, im = ar * br + ai * bi, ai * br - ar * bi
            cross_re = re if cross_re is None else cross_re + re
            cross_im = im if cross_im is None else cross_im + im
        cross = jnp.concatenate([cross_re, cross_im], axis=1).astype(jnp.bfloat16)
        out_ref[0] += jnp.dot(cross, lag_ref[0], preferred_element_type=jnp.float32)

    @pl.when(late == 0)
    def _():
        work(g_ref, h_ref)

    @pl.when(late == 1)
    def _():
        work(h_ref, g_ref)


def pair_partials(place, idx, g, h, lag):
    spectra = pl.BlockSpec((ROW, 1, SEG, CH, 256), lambda u, y: (0, u, 0, 0, 0))
    return pl.pallas_call(
        pair_kernel,
        out_shape=jax.ShapeDtypeStruct((2, 512, LAGS), jnp.float32),
        grid_spec=pltpu.PrefetchScalarGridSpec(
            num_scalar_prefetch=1,
            grid=(8,),
            in_specs=[
                pl.BlockSpec((1, 512, 2), lambda u, y: (u // 4, 0, 0)),
                spectra,
                spectra,
                pl.BlockSpec((1, 256, LAGS), lambda u, y: (8 * y[0] + u, 0, 0)),
            ],
            out_specs=pl.BlockSpec((1, 512, LAGS), lambda u, y: (u // 4, 0, 0)),
            scratch_shapes=[pltpu.VMEM((512, 128), jnp.bfloat16), pltpu.VMEM((512, 256), jnp.bfloat16)],
        ),
        compiler_params=pltpu.CompilerParams(vmem_limit_bytes=48 * 2**20),
    )(place, idx, g, h, lag)


def body(traces, alive, pair_chan, lag_window):
    n = lax.axis_size("chan")
    me = lax.axis_index("chan")
    row, y = me // ROW, me % ROW
    rows = n // ROW
    groups = [[r * ROW + k for k in range(ROW)] for r in range(rows)]
    live = jnp.broadcast_to(alive.astype(jnp.float32)[:, None], (CH, 128))
    spectra = whiten(traces.reshape(CH * SEG, SAMP), live, jnp.asarray(second_table()))
    g = lax.all_to_all(
        spectra.reshape(ROW, 8, SEG, CH, 256), "chan", split_axis=0, concat_axis=0, axis_index_groups=groups
    )
    back = [(i, (i - ROW) % n) for i in range(n)]
    ahead = [(i, (i + ROW) % n) for i in range(n)]
    h = jnp.concatenate(
        [lax.ppermute(g[:, :4], "chan", back), lax.ppermute(g[:, 4:], "chan", ahead)], axis=1
    )
    all_pairs = lax.all_gather(pair_chan, "chan", tiled=True)
    before = (row + rows - 1) % rows
    idx = jnp.stack(
        [
            lax.dynamic_slice_in_dim(all_pairs, row * 512, 512) - row * 128,
            lax.dynamic_slice_in_dim(all_pairs, before * 512, 512) - before * 128,
        ]
    )
    partial = pair_partials(y[None], idx, g, h, jnp.asarray(lag_table()))
    partial = partial.astype(jnp.bfloat16).reshape(2, ROW, SEG, 32, LAGS)
    partial = lax.psum_scatter(partial, "chan", scatter_dimension=1, axis_index_groups=groups)
    partial = lax.psum_scatter(partial, "seg", scatter_dimension=1)
    lagged = (partial[0] + lax.ppermute(partial[1], "chan", back)).astype(jnp.float32)
    lag_value = jnp.abs(jnp.arange(LAGS, dtype=jnp.int32) - LAGS // 2)
    keep = lag_value[None, :] <= lag_window[:, None]
    return jnp.where(keep, lagged, jnp.zeros_like(lagged))


def solution(mesh):
    in_specs = (P("chan", "seg", None), P("chan"), P("chan", None), P(("chan", "seg")))
    out_specs = P(("chan", "seg"), None)
    return jax.shard_map(body, mesh=mesh, in_specs=in_specs, out_specs=out_specs, check_vma=False)
```

time: 1150 us -> 239 us (0.21); the launches traced: 1140 us -> 238 us
  other arithmetic: 623 us -> 5.37 us
  waiting for transfers between devices: 365 us -> 79.3 us
  blocking collectives: 0 us -> 112 us
  local copies, waits for them, and re-layouts: 87 us -> 7.56 us
  matrix products: 42 us -> 0 us
  Pallas kernels: 0 us -> 13.9 us
    another operation x10 -> x2, other arithmetic: 547 us -> 0.01 us  [body(): jnp.stack([lax.dynamic_slice_in_dim(all_pairs, row * 512, 512) - row * 12...]
    ppermute x4 -> x3, waiting for transfers between devices: 213 us -> 1.02 us  [the longest x1 1.02 us: body(): lax.ppermute(partial[1], 'chan', back)]
    reduce_scatter x1, waiting for transfers between devices: 151 us -> 34.1 us  [body(): lax.psum_scatter(partial, 'chan', scatter_dimension=1, axis_index_groups=...]
    all_gather x0 -> x1, blocking collectives: none -> 81.5 us  [body(): all_pairs = lax.all_gather(pair_chan, 'chan', tiled=True)]
    unnamed x1 -> x3, waiting for transfers between devices: 0.02 us -> 44.1 us
    dot_general x9 -> x0, matrix products: 42 us -> none  [the longest x8 29.9 us: whiten_rows(): spectrum = jnp.dot(trace_rows, table, preferred_element_type=jnp.float32)]
    cos x1 -> x0, other arithmetic: 34.6 us -> none  [lag_table(): return jnp.concatenate([jnp.cos(angle), -jnp.sin(angle)], axis=0)]
    all_to_all x0 -> x1, blocking collectives: none -> 30.2 us  [body(): lax.all_to_all(spectra.reshape(ROW, 8, SEG, CH, 256), 'chan', split_axis=...]
  transfers between devices with their start and end apart: 5 -> 5, of which waited for: 3 -> 3; matrix products, arithmetic and copies ran while one was open for 4% -> 0% of each run, Pallas kernels for 0% -> 0%
where the time goes in v1:
time: 239 us; the launch traced here: 238 us
  blocking collectives  112 us (47%)
  waiting for transfers between devices  79.3 us (33%)
  Pallas kernels  13.9 us (6%)
  between operations  13.5 us (6%)
  local copies, waits for them, and re-layouts  7.56 us (3%)
  starting transfers between devices  6.38 us (3%)
  other arithmetic  5.37 us (2%)
    all_gather x1, blocking collectives, body(): all_pairs = lax.all_gather(pair_chan, 'chan', tiled=True)  81.5 us
    unnamed x3, waiting for transfers between devices  44.1 us
    reduce_scatter x1, waiting for transfers between devices, body(): lax.psum_scatter(partial, 'chan', scatter_dimension=1, axis_index_groups=...  34.1 us
    all_to_all x1, blocking collectives, body(): lax.all_to_all(spectra.reshape(ROW, 8, SEG, CH, 256), 'chan', split_axis=...  30.2 us
    pallas_call x1, Pallas kernels, pair_partials(): pl.pallas_call(pair_kernel, out_shape=jax.ShapeDtypeStruct((2, 512, LAGS)...  9.01 us
    pallas_call x1, Pallas kernels, whiten(): pl.pallas_call(whiten_kernel, out_shape=jax.ShapeDtypeStruct((UNITS, SEG,...  4.91 us
  transfers between devices with their start and end apart: 5, of which 3 were waited for; matrix products, arithmetic and copies ran while one was open for 0% of the time, Pallas kernels for 0%

profile of v1, /device:TPU:1, one launch (start us, length us, event | category | flops | bytes accessed | tf_op | source)
XLA Modules:
  0.0 237.7 jit_solution(1214603124454169532)
XLA Ops:
  6.5 0.0 copy-start.2
  6.5 0.0 reduce-scatter.5.cloned.1.call-start
  6.5 2.5 %reshape.20.x_ref = bf16[128,8192]{1,0:T(8,128)(2,1)S(1)} reshape(bf16[32,4,8192]{2,1,0:T(4,128)(2,1)} %param.6) | data formatting | bytes 4194304 | tf_op jit(solution)/shard_map/reshape | solution.py:213
  9.1 0.0 copy-done.2
  9.1 0.1 broadcast_in_dim.7.live_ref
  9.2 4.9 %shard_map.64 = bf16[32,4,32,256]{3,2,1,0:T(8,128)(2,1)S(1)} custom-call(bf16[128,8192]{1,0:T(8,128)(2,1)S(1)} %reshape.20.x_ref, f32[32,128]{1,0:T(8,128)S(1)} %broadcast_in_dim.7.live_ref, bf16[32,256,256]{2,1,0:T(8,128)(2,1)} %constant.61.clone.table_hbm), custom_call_target="tpu_custom_call" | custom-call | tf_op jit(solution)/shard_map/pallas_call | solution.py:126
  14.1 30.2 %all_to_all.5.g_ref = bf16[4,8,4,32,256]{4,3,2,1,0:T(8,128)(2,1)S(1)} all-to-all(bf16[4,8,4,32,256]{4,3,2,1,0:T(8,128)(2,1)S(1)} %bitcast.23), channel_id=1, replica_groups={{0,4,8,12},{16,20,24,28},{32,36,40,44},{48,52,56,60},{64,68,72,76},{80,..., dimensions={0} | all-to-all | bytes 4194304 | tf_op jit(solution)/shard_map/all_to_all | solution.py:214
  44.3 0.0 copy-start
  44.3 1.6 fusion.1
  45.9 3.8 %collective-permute-start = (bf16[4,4,4,32,256]{4,3,2,1,0:T(8,128)(2,1)}, bf16[4,4,4,32,256]{4,3,2,1,0:T(8,128)(2,1)}, u32[]{:S(2)}, u32[]{:S(2)}) collective-permute-start(bf16[4,4,4,32,256]{4,3,2,1,0:T(8,128)(2,1)} %get-tuple-element.5), channel_id=1, source_target_pairs={{0,112},{4,116},{8,120},{12,124},{16,0},{20,4},{24,8},{28,12},{32,... | collective-permute-start | bytes 3145736 | tf_op jit(solution)/shard_map/ppermute | solution.py:220
  49.7 0.0 collective-permute-start.1
  49.7 0.0 copy-done
  49.7 81.5 %all_gather.3 = s32[4096,2]{0,1:T(2,128)S(1)} all-gather(s32[128,2]{0,1:T(2,128)S(1)} %copy-done), channel_id=1, replica_groups=mesh['chan'=32,'seg'=4] {'chan'}, dimensions={0}, use_global_device_ids=true | all-gather | bytes 33792 | tf_op jit(solution)/shard_map/all_gather | solution.py:222
  131.2 0.2 copy.9.idx_ref
  131.5 0.0 collective-permute-done
  131.5 0.0 collective-permute-done.1
  131.5 3.1 %pad_maximum_fusion.h_ref = bf16[4,8,4,32,256]{4,3,2,1,0:T(8,128)(2,1)} fusion(bf16[4,4,4,32,256]{4,3,2,1,0:T(8,128)(2,1)} %collective-permute-done.1, bf16[4,4,4,32,256]{4,3,2,1,0:T(8,128)(2,1)} %collective-permute-done), kind=kLoop, calls=%fused_computation | loop fusion | flops 1048576 | bytes 4194304 | tf_op jit(solution)/shard_map/concatenate | solution.py:219
  134.6 9.0 %shard_map.65 = f32[2,512,512]{2,1,0:T(8,128)S(1)} custom-call(s32[1]{0:T(128)} %bitcast.6.place, s32[2,512,2]{2,1,0:T(8,128)S(1)} %copy.9.idx_ref, bf16[4,8,4,32,256]{4,3,2,1,0:T(8,128)(2,1)S(1)} %all_to_all.5.g_ref, bf16[4,8,4,32,256]{4,3,2,1,0:T(8,128)(2,1)} %pad_maximum_fusion.h_ref, bf16[32,256,512]{2,1,0:T(8,128)(2,1)} %constant.62.clone.lag_ref), custom_call_target="tpu_custom_call" | custom-call | tf_op jit(solution)/shard_map/pallas_call | solution.py:187
  143.6 0.1 convert_element_type.10
  143.7 0.0 copy-start.3
  143.7 0.0 copy-start.1
  143.7 1.0 copy.10
  144.8 0.0 reduce-scatter.5.cloned.1.call-update
  144.8 0.0 all-reduce.3.cloned.1.call-start
  144.9 34.1 %reduce-scatter.5.cloned.1.call-done = bf16[2,1,4,32,512]{4,3,2,0,1:T(8,128)(2,1)} async-done(((bf16[2,4,4,32,512]{4,3,2,0,1:T(8,128)(2,1)}), bf16[2,1,4,32,512]{4,3,2,0,1:T(8,128)(2,1)}) %reduce-scatter.5.cloned.1.call-update) | async-done | bytes 262160 | tf_op jit(solution)/shard_map/reduce_scatter | solution.py:232
  178.9 0.0 all-reduce.3.cloned.1.call-update
  179.0 0.0 copy-done.3
  179.0 0.7 dynamic-slice
  179.6 44.1 %all-reduce.3.cloned.1.call-done = bf16[2,4,32,512]{3,2,1,0:T(8,128)(2,1)} async-done(((bf16[2,4,32,512]{3,2,1,0:T(8,128)(2,1)}), bf16[2,4,32,512]{3,2,1,0:T(8,128)(2,1)}) %all-reduce.3.cloned.1.call-update) | async-done | bytes 262160
  223.8 1.5 dynamic-slice_bitcast_fusion
  225.2 2.5 %collective-permute-start.2 = (bf16[32,512]{1,0:T(8,128)(2,1)S(1)}, bf16[32,512]{1,0:T(8,128)(2,1)S(1)}, u32[]{:S(2)}, u32[]{:S(2)}) collective-permute-start(bf16[32,512]{1,0:T(8,128)(2,1)S(1)} %dynamic-slice_bitcast_fusion), channel_id=1, source_target_pairs={{0,112},{4,116},{8,120},{12,124},{16,0},{20,4},{24,8},{28,12},{32,... | collective-permute-start | bytes 98312 | tf_op jit(solution)/shard_map/ppermute | solution.py:234
  227.7 1.0 collective-permute-done.2
  228.7 0.0 copy-done.1
  228.7 2.2 convert_select_fusion
  (4 shorter events, 0.0 us)
Async XLA Ops:
  6.5 2.6 %copy-start.2 = (s32[32]{0:T(128)S(1)}, s32[32]{0:T(128)}, u32[]{:S(2)}) copy-start(s32[32]{0:T(128)} %param.7) | copy-start | bytes 388
  6.5 172.4 %reduce-scatter.5.cloned.1.call-start = ((), (), s32[]{:S(2)}) async-start(), calls=%async_computation.2 | async-start | bytes 1310720 | tf_op jit(solution)/shard_map/reduce_scatter | solution.py:232
  44.3 5.4 %copy-start = (s32[128,2]{0,1:T(2,128)S(1)}, s32[128,2]{0,1:T(2,128)}, u32[]{:S(2)}) copy-start(s32[128,2]{0,1:T(2,128)} %param.8) | copy-start | bytes 3076
  45.9 85.6 %collective-permute-start = (bf16[4,4,4,32,256]{4,3,2,1,0:T(8,128)(2,1)}, bf16[4,4,4,32,256]{4,3,2,1,0:T(8,128)(2,1)}, u32[]{:S(2)}, u32[]{:S(2)}) collective-permute-start(bf16[4,4,4,32,256]{4,3,2,1,0:T(8,128)(2,1)} %get-tuple-element.5), channel_id=1, source_target_pairs={{0,112},{4,116},{8,120},{12,124},{16,0},{20,4},{24,8},{28,12},{32,... | collective-permute-start | bytes 3145736 | tf_op jit(solution)/shard_map/ppermute | solution.py:220
  49.7 81.8 %collective-permute-start.1 = (bf16[4,4,4,32,256]{4,3,2,1,0:T(8,128)(2,1)}, bf16[4,4,4,32,256]{4,3,2,1,0:T(8,128)(2,1)}, u32[]{:S(2)}, u32[]{:S(2)}) collective-permute-start(bf16[4,4,4,32,256]{4,3,2,1,0:T(8,128)(2,1)} %get-tuple-element.6), channel_id=1, source_target_pairs={{0,16},{4,20},{8,24},{12,28},{16,32},{20,36},{24,40},{28,44},{32,4... | collective-permute-start | bytes 3145736 | tf_op jit(solution)/shard_map/ppermute | solution.py:220
  143.7 35.2 %copy-start.3 = (u32[128]{0:T(128)S(1)}, u32[128]{0:T(128)}, u32[]{:S(2)}) copy-start(u32[128]{0:T(128)} %constant.66) | copy-start | bytes 1540
  143.7 85.0 %copy-start.1 = (s32[32]{0:T(128)S(1)}, s32[32]{0:T(128)}, u32[]{:S(2)}) copy-start(s32[32]{0:T(128)} %param.9) | copy-start | bytes 388
  144.8 79.0 %all-reduce.3.cloned.1.call-start = ((), (), s32[]{:S(2)}) async-start(), calls=%async_computation.3 | async-start | bytes 524288
  225.2 3.5 %collective-permute-start.2 = (bf16[32,512]{1,0:T(8,128)(2,1)S(1)}, bf16[32,512]{1,0:T(8,128)(2,1)S(1)}, u32[]{:S(2)}, u32[]{:S(2)}) collective-permute-start(bf16[32,512]{1,0:T(8,128)(2,1)S(1)} %dynamic-slice_bitcast_fusion), channel_id=1, source_target_pairs={{0,112},{4,116},{8,120},{12,124},{16,0},{20,4},{24,8},{28,12},{32,... | collective-permute-start | bytes 98312 | tf_op jit(solution)/shard_map/ppermute | solution.py:234
Sparse Core Ops, SparseCore 0:
  144.9 33.9 reduce-scatter.4
  181.6 42.1 all-reduce.2

commit v2 on v1

--- a/solution.py
+++ b/solution.py
@@ -18,6 +18,9 @@
 CH = 32
 SEG = 4
 EPS = 1e-06
+AHEAD = 3
+DELAY = 3
+MESH = pl.DeviceIdType.MESH
 
 
 def unit_bins():
@@ -143,98 +146,258 @@
     )(rows, live, table)
 
 
-def pair_kernel(place, idx_ref, g_ref, h_ref, lag_ref, out_ref, first_pick, second_pick):
-    unit = pl.program_id(0)
-    late = unit // 4
-
-    @pl.when(unit % 4 == 0)
-    def _():
-        lanes = lax.broadcasted_iota(jnp.int32, (512, 128), 1)
-        i = idx_ref[0, :, 0:1]
-        j = idx_ref[0, :, 1:2]
-        first_pick[...] = jnp.where(lanes == i, 1.0, 0.0).astype(jnp.bfloat16)
-        second_pick[:, 0:128] = jnp.where(lanes == j, 1.0, 0.0).astype(jnp.bfloat16)
-        second_pick[:, 128:256] = jnp.where(lanes + 128 == j, 1.0, 0.0).astype(jnp.bfloat16)
-        out_ref[...] = jnp.zeros_like(out_ref)
-
-    def side(ref, s):
-        return jnp.concatenate([ref[b, 0, s] for b in range(ROW)], axis=0)
-
-    def work(near, far):
+def exchange_kernel(
+    rows, pair_ref, window_ref, w_ref, lag_hbm, out_ref,
+    both, lag, idx, first_pick, second_pick, total, half_out, half_in, piece, got,
+    y_send, y_recv, x_send, x_recv, idx_send, idx_recv, half_send, half_recv, sum_send, sum_recv, local,
+):
+    me, seg = lax.axis_index("chan"), lax.axis_index("seg")
+    row, y = me // ROW, me % ROW
+    zh, core = seg // 2, seg % 2
+    before, after = (row + rows - 1) % rows, (row + 1) % rows
+    mine = y * 2 + zh
+
+    def at(r, q):
+        return (r * ROW + q // 2, (q % 2) * 2 + core)
+
+    def remote(src, dst, send, recv, device):
+        return pltpu.make_async_remote_copy(
+            src_ref=src, dst_ref=dst, send_sem=send, recv_sem=recv, device_id=device, device_id_type=MESH
+        )
+
+    sibling = (me, zh * 2 + 1 - core)
+    barrier = pltpu.get_barrier_semaphore()
+
+    def greet(device):
+        pl.semaphore_signal(barrier, inc=1, device_id=device, device_id_type=MESH)
+
+    greet(sibling)
+    for k in range(8):
+        if k:
+            greet(at(row, (mine + k) % 8))
+        greet(at(before, (mine + k) % 8))
+        greet(at(after, (mine + k) % 8))
+    pl.semaphore_wait(barrier, 24)
+
+    fetch = pltpu.make_async_copy(lag_hbm.at[pl.ds(8 * y, 8)], lag, local.at[0])
+    keep_own = pltpu.make_async_copy(w_ref.at[y], both.at[0, :, :, y], local.at[1])
+
+    def y_copy(d, u):
+        to = (y + d) % ROW
+        return remote(
+            w_ref.at[to, u], both.at[0, u, :, y], y_send.at[d - 1, u], y_recv.at[d - 1, u], (row * ROW + to, seg)
+        )
+
+    def y_arrival(d, u):
+        source = (y + ROW - d) % ROW
+        return remote(
+            w_ref.at[y, u], both.at[0, u, :, source], y_send.at[d - 1, u], y_recv.at[d - 1, u],
+            (row * ROW + source, seg),
+        )
+
+    def x_copy(u):
+        to = (row + rows - 1 + 2 * (u // 4)) % rows
+        return remote(both.at[0, u], both.at[1, u], x_send.at[u], x_recv.at[u], (to * ROW + y, seg))
+
+    def unit_of(step):
+        return (step % 2) * 4 + step // 2
+
+    def start_y(step):
+        for d in (2, 1, 3):
+            y_copy(d, unit_of(step)).start()
+
+    for step in range(AHEAD):
+        start_y(step)
+    keep_own.start()
+    fetch.start()
+
+    own_idx = [pltpu.make_async_copy(pair_ref, idx.at[y], local.at[2])]
+    sends, waits = [], []
+    for d in range(1, ROW):
+        sends.append(
+            remote(pair_ref, idx.at[y], idx_send.at[d], idx_recv.at[d], (row * ROW + (y + d) % ROW, seg))
+        )
+        waits.append(
+            remote(pair_ref, idx.at[(y + ROW - d) % ROW], idx_send.at[d], idx_recv.at[d],
+                   (row * ROW + (y + d) % ROW, seg))
+        )
+    for d in range(ROW):
+        sends.append(
+            remote(pair_ref, idx.at[ROW + y], idx_send.at[4 + d], idx_recv.at[4 + d],
+                   (after * ROW + (y + d) % ROW, seg))
+        )
+        waits.append(
+            remote(pair_ref, idx.at[ROW + (y + ROW - d) % ROW], idx_send.at[4 + d], idx_recv.at[4 + d],
+                   (after * ROW + (y + d) % ROW, seg))
+        )
+    for copy in own_idx + sends:
+        copy.start()
+    total[...] = jnp.zeros_like(total)
+    own_idx[0].wait()
+    for copy in sends:
+        copy.wait_send()
+    for copy in waits:
+        copy.wait_recv()
+
+    channel = lax.broadcasted_iota(jnp.int32, (128, 128), 0)
+
+    def make_picks(slot, carry):
+        side = slot // ROW
+        base = jnp.where(side == 0, row, before) * (ROW * CH)
+        at_rows = pl.ds(pl.multiple_of((slot % ROW) * 128, 128), 128)
+
+        def picks(which, shift):
+            hit = channel + (base + shift) == idx[slot, which : which + 1, :]
+            return jnp.where(hit, 1.0, 0.0).T.astype(jnp.bfloat16)
+
+        first_pick[side, at_rows, :] = picks(0, 0)
+        second_pick[side, at_rows, 0:128] = picks(1, 0)
+        second_pick[side, at_rows, 128:256] = picks(1, 128)
+        return carry
+
+    lax.fori_loop(0, 8, make_picks, 0)
+    keep_own.wait()
+    fetch.wait()
+
+    def correlate(u):
+        late = u // 4
         cross_re = cross_im = None
         for s in range(SEG):
-            own, other = side(near, s), side(far, s)
-            a = jnp.dot(first_pick[...], own, preferred_element_type=jnp.float32)
-            b = jnp.dot(second_pick[...], jnp.concatenate([own, other], axis=0), preferred_element_type=jnp.float32)
+            near = both[late, u, s].reshape(128, 256)
+            far = both[1 - late, u, s].reshape(128, 256)
+            a = jnp.dot(first_pick[late], near, preferred_element_type=jnp.float32)
+            b = jnp.dot(
+                second_pick[late], jnp.concatenate([near, far], axis=0), preferred_element_type=jnp.float32
+            )
             ar, ai, br, bi = a[:, :128], a[:, 128:], b[:, :128], b[:, 128:]
             re, im = ar * br + ai * bi, ai * br - ar * bi
             cross_re = re if cross_re is None else cross_re + re
             cross_im = im if cross_im is None else cross_im + im
         cross = jnp.concatenate([cross_re, cross_im], axis=1).astype(jnp.bfloat16)
-        out_ref[0] += jnp.dot(cross, lag_ref[0], preferred_element_type=jnp.float32)
-
-    @pl.when(late == 0)
-    def _():
-        work(g_ref, h_ref)
-
-    @pl.when(late == 1)
-    def _():
-        work(h_ref, g_ref)
-
-
-def pair_partials(place, idx, g, h, lag):
-    spectra = pl.BlockSpec((ROW, 1, SEG, CH, 256), lambda u, y: (0, u, 0, 0, 0))
+        total[late] += jnp.dot(cross, lag[u], preferred_element_type=jnp.float32)
+
+    def advance(step, carry):
+        @pl.when(step + AHEAD < 8)
+        def _():
+            start_y(step + AHEAD)
+
+        @pl.when(step < 8)
+        def _():
+            u = unit_of(step)
+            for d in (1, 3, 2):
+                y_arrival(d, u).wait_recv()
+            x_copy(u).start()
+
+        @pl.when(step >= DELAY)
+        def _():
+            u = unit_of(step - DELAY)
+            x_copy(u).wait_recv()
+            correlate(u)
+
+        return carry
+
+    lax.fori_loop(0, 8 + DELAY, advance, 0)
+
+    def sent(u, carry):
+        for d in (1, 2, 3):
+            y_copy(d, u).wait_send()
+        x_copy(u).wait_send()
+        return carry
+
+    lax.fori_loop(0, 8, sent, 0)
+
+    def rows_of(q, c):
+        return pl.ds(pl.multiple_of(q * 64 + c * 32, 32), 32)
+
+    def half_copy(side):
+        return remote(half_out.at[side], half_in.at[side], half_send.at[side], half_recv.at[side], sibling)
+
+    for side in range(2):
+        def pack(q, carry, side=side):
+            half_out[side, q] = total[side, rows_of(q, 1 - core), :].astype(jnp.bfloat16)
+            return carry
+
+        lax.fori_loop(0, 8, pack, 0)
+        half_copy(side).start()
+
+    def sum_copy(side, k):
+        to = row if side == 0 else before
+        q = (mine + k) % 8
+        return remote(piece.at[side, q], got.at[side, k], sum_send.at[side, k], sum_recv.at[side, k], at(to, q))
+
+    for side in range(2):
+        half_copy(side).wait_recv()
+
+        def combine(q, carry, side=side):
+            value = total[side, rows_of(q, core), :] + half_in[side, q].astype(jnp.float32)
+            piece[side, q] = value.astype(jnp.bfloat16)
+            return carry
+
+        lax.fori_loop(0, 8, combine, 0)
+        for k in range(1 - side, 8):
+            sum_copy(side, k).start()
+    for side in range(2):
+        half_copy(side).wait_send()
+
+    result = piece[0, mine].astype(jnp.float32)
+    for side in range(2):
+        for k in range(1 - side, 8):
+            sum_copy(side, k).wait_recv()
+            result = result + got[side, k].astype(jnp.float32)
+    diagonal = lax.broadcasted_iota(jnp.int32, (32, 32), 0) == lax.broadcasted_iota(jnp.int32, (32, 32), 1)
+    widest = jnp.sum(jnp.where(diagonal, window_ref[...].astype(jnp.float32), 0.0), axis=1, keepdims=True)
+    lags = jnp.abs(lax.broadcasted_iota(jnp.int32, (32, LAGS), 1) - LAGS // 2).astype(jnp.float32)
+    out_ref[...] = jnp.where(lags <= widest, result, 0.0)
+    for side in range(2):
+        for k in range(1 - side, 8):
+            sum_copy(side, k).wait_send()
+
+
+def exchange(rows, pairs, window, spectra, lag):
+    dma = pltpu.SemaphoreType.DMA
+    vmem = pl.BlockSpec(memory_space=pltpu.VMEM)
+    pieces = pltpu.VMEM((2, 8, 32, LAGS), jnp.bfloat16)
     return pl.pallas_call(
-        pair_kernel,
-        out_shape=jax.ShapeDtypeStruct((2, 512, LAGS), jnp.float32),
-        grid_spec=pltpu.PrefetchScalarGridSpec(
-            num_scalar_prefetch=1,
-            grid=(8,),
-            in_specs=[
-                pl.BlockSpec((1, 512, 2), lambda u, y: (u // 4, 0, 0)),
-                spectra,
-                spectra,
-                pl.BlockSpec((1, 256, LAGS), lambda u, y: (8 * y[0] + u, 0, 0)),
-            ],
-            out_specs=pl.BlockSpec((1, 512, LAGS), lambda u, y: (u // 4, 0, 0)),
-            scratch_shapes=[pltpu.VMEM((512, 128), jnp.bfloat16), pltpu.VMEM((512, 256), jnp.bfloat16)],
+        functools.partial(exchange_kernel, rows),
+        out_shape=jax.ShapeDtypeStruct((32, LAGS), jnp.float32),
+        in_specs=[vmem, vmem, vmem, pl.BlockSpec(memory_space=pl.ANY)],
+        out_specs=vmem,
+        scratch_shapes=[
+            pltpu.VMEM((2, 8, SEG, ROW, CH, 256), jnp.bfloat16),
+            pltpu.VMEM((8, 256, LAGS), jnp.bfloat16),
+            pltpu.VMEM((8, 2, 128), jnp.int32),
+            pltpu.VMEM((2, 512, 128), jnp.bfloat16),
+            pltpu.VMEM((2, 512, 256), jnp.bfloat16),
+            pltpu.VMEM((2, 512, LAGS), jnp.float32),
+            pieces,
+            pieces,
+            pieces,
+            pieces,
+            dma((3, 8)),
+            dma((3, 8)),
+            dma((8,)),
+            dma((8,)),
+            dma((8,)),
+            dma((8,)),
+            dma((2,)),
+            dma((2,)),
+            dma((2, 8)),
+            dma((2, 8)),
+            dma((3,)),
+        ],
+        compiler_params=pltpu.CompilerParams(
+            collective_id=0, has_side_effects=True, vmem_limit_bytes=48 * 2**20
         ),
-        compiler_params=pltpu.CompilerParams(vmem_limit_bytes=48 * 2**20),
-    )(place, idx, g, h, lag)
+    )(pairs, window, spectra, lag)
 
 
 def body(traces, alive, pair_chan, lag_window):
-    n = lax.axis_size("chan")
-    me = lax.axis_index("chan")
-    row, y = me // ROW, me % ROW
-    rows = n // ROW
-    groups = [[r * ROW + k for k in range(ROW)] for r in range(rows)]
+    rows = lax.axis_size("chan") // ROW
     live = jnp.broadcast_to(alive.astype(jnp.float32)[:, None], (CH, 128))
     spectra = whiten(traces.reshape(CH * SEG, SAMP), live, jnp.asarray(second_table()))
-    g = lax.all_to_all(
-        spectra.reshape(ROW, 8, SEG, CH, 256), "chan", split_axis=0, concat_axis=0, axis_index_groups=groups
+    return exchange(
+        rows, pair_chan.T, lag_window[None], spectra.reshape(ROW, 8, SEG, CH, 256), jnp.asarray(lag_table())
     )
-    back = [(i, (i - ROW) % n) for i in range(n)]
-    ahead = [(i, (i + ROW) % n) for i in range(n)]
-    h = jnp.concatenate(
-        [lax.ppermute(g[:, :4], "chan", back), lax.ppermute(g[:, 4:], "chan", ahead)], axis=1
-    )
-    all_pairs = lax.all_gather(pair_chan, "chan", tiled=True)
-    before = (row + rows - 1) % rows
-    idx = jnp.stack(
-        [
-            lax.dynamic_slice_in_dim(all_pairs, row * 512, 512) - row * 128,
-            lax.dynamic_slice_in_dim(all_pairs, before * 512, 512) - before * 128,
-        ]
-    )
-    partial = pair_partials(y[None], idx, g, h, jnp.asarray(lag_table()))
-    partial = partial.astype(jnp.bfloat16).reshape(2, ROW, SEG, 32, LAGS)
-    partial = lax.psum_scatter(partial, "chan", scatter_dimension=1, axis_index_groups=groups)
-    partial = lax.psum_scatter(partial, "seg", scatter_dimension=1)
-    lagged = (partial[0] + lax.ppermute(partial[1], "chan", back)).astype(jnp.float32)
-    lag_value = jnp.abs(jnp.arange(LAGS, dtype=jnp.int32) - LAGS // 2)
-    keep = lag_value[None, :] <= lag_window[:, None]
-    return jnp.where(keep, lagged, jnp.zeros_like(lagged))
 
 
 def solution(mesh):

time: 239 us -> 66.2 us (0.28)
  blocking collectives: 112 us -> 0 us
  waiting for transfers between devices: 79.3 us -> 0 us
  Pallas kernels: 13.9 us -> 62 us
  between operations: 13.5 us -> 0.06 us
  starting transfers between devices: 6.38 us -> 0 us
  other arithmetic: 5.37 us -> 0.66 us
  local copies, waits for them, and re-layouts: 7.56 us -> 3.25 us
    all_gather x1 -> x0, blocking collectives: 81.5 us -> none  [body(): all_pairs = lax.all_gather(pair_chan, 'chan', tiled=True)]
    pallas_call x1, Pallas kernels: 9.01 us -> 57.1 us  [exchange(): pl.pallas_call(functools.partial(exchange_kernel, rows), out_shape=jax.Sh...]
    unnamed x3 -> x0, waiting for transfers between devices: 44.1 us -> none
    reduce_scatter x1 -> x0, waiting for transfers between devices: 34.1 us -> none  [body(): lax.psum_scatter(partial, 'chan', scatter_dimension=1, axis_index_groups=...]
    all_to_all x1 -> x0, blocking collectives: 30.2 us -> none  [body(): lax.all_to_all(spectra.reshape(ROW, 8, SEG, CH, 256), 'chan', split_axis=...]
    ppermute x3 -> x0, starting transfers between devices: 6.34 us -> none  [the longest x1 3.83 us: body(): lax.ppermute(g[:, :4], 'chan', back)]
    concatenate x1 -> x0, other arithmetic: 3.07 us -> none  [body(): jnp.concatenate([lax.ppermute(g[:, :4], 'chan', back), lax.ppermute(g[:,...]
  transfers between devices with their start and end apart: 5 -> 0, of which waited for: 3 -> 0; matrix products, arithmetic and copies ran while one was open for 0% -> 0% of each run, Pallas kernels for 0% -> 0%
where the time goes in v2:
time: 66.2 us; the launch traced here: 66 us
  Pallas kernels  62 us (94%)
  local copies, waits for them, and re-layouts  3.25 us (5%)
    pallas_call x1, Pallas kernels, exchange(): pl.pallas_call(functools.partial(exchange_kernel, rows), out_shape=jax.Sh...  57.1 us
    pallas_call x1, Pallas kernels, whiten(): pl.pallas_call(whiten_kernel, out_shape=jax.ShapeDtypeStruct((UNITS, SEG,...  4.91 us
    reshape x1, local copies, waits for them, and re-layouts, body(): traces.reshape(CH * SEG, SAMP)  2.54 us

profile of v2, /device:TPU:1, one launch (start us, length us, event | category | flops | bytes accessed | tf_op | source)
XLA Modules:
  0.0 66.0 jit_solution(3496201984770282123)
XLA Ops:
  0.0 0.7 convert_element_type.3
  0.7 0.1 broadcast_in_dim.10.live_ref
  0.7 2.5 %reshape.7.x_ref = bf16[128,8192]{1,0:T(8,128)(2,1)S(1)} reshape(bf16[32,4,8192]{2,1,0:T(4,128)(2,1)} %param.6) | data formatting | bytes 4194304 | tf_op jit(solution)/shard_map/reshape | solution.py:397
  3.3 0.0 copy-start
  3.3 0.0 copy-start.1
  3.3 4.9 %shard_map.64 = bf16[32,4,32,256]{3,2,1,0:T(8,128)(2,1)S(1)} custom-call(bf16[128,8192]{1,0:T(8,128)(2,1)S(1)} %reshape.7.x_ref, f32[32,128]{1,0:T(8,128)S(1)} %broadcast_in_dim.10.live_ref, bf16[32,256,256]{2,1,0:T(8,128)(2,1)} %constant.4.clone.table_hbm), custom_call_target="tpu_custom_call" | custom-call | tf_op jit(solution)/shard_map/pallas_call | solution.py:129
  8.2 0.0 copy-done
  8.2 0.0 copy-done.1
  8.2 57.1 %shard_map.65 = f32[32,512]{1,0:T(8,128)S(1)} custom-call(s32[2,128]{1,0:T(2,128)S(1)} %bitcast.4, s32[1,32]{1,0:T(1,128)S(1)} %bitcast.5, bf16[4,8,4,32,256]{4,3,2,1,0:T(8,128)(2,1)S(1)} %bitcast.3, bf16[32,256,512]{2,1,0:T(8,128)(2,1)} %constant.5.clone.lag_hbm), custom_call_target="tpu_custom_call" | custom-call | tf_op jit(solution)/shard_map/pallas_call | solution.py:360
  65.4 0.6 copy.8
Async XLA Ops:
  3.3 4.9 %copy-start = (s32[128,2]{0,1:T(2,128)S(1)}, s32[128,2]{0,1:T(2,128)}, u32[]{:S(2)}) copy-start(s32[128,2]{0,1:T(2,128)} %param.8) | copy-start | bytes 3076
  3.3 4.9 %copy-start.1 = (s32[32]{0:T(128)S(1)}, s32[32]{0:T(128)}, u32[]{:S(2)}) copy-start(s32[32]{0:T(128)} %param.9) | copy-start | bytes 388

commit v3 on v2

v3 whole, which is shorter than its diff:
```python
import functools
import math

import jax
import jax.numpy as jnp
import numpy as np
from jax import lax
from jax.experimental import pallas as pl
from jax.experimental.pallas import tpu as pltpu
from jax.sharding import PartitionSpec as P

FREQ = 4096
SAMP = 8192
BAND = 64
LAGS = 512
UNITS = 32
ROW = 4
CH = 32
SEG = 4
EPS = 1e-06
AHEAD = 4
DELAY = 4
PICKS = 6
MESH = pl.DeviceIdType.MESH


def unit_bins():
    u = np.arange(UNITS)[:, None]
    lane = np.arange(128)[None, :]
    low = np.where(lane < 64, u, np.where(u == 0, 32, 64 - u))
    return low + 64 * (lane % 64)


def second_table():
    bins = unit_bins()[:, None, :]
    t2 = np.arange(128)[None, :, None]
    angle = 2.0 * np.pi * ((t2 * bins) % SAMP) / SAMP
    c, s = np.cos(angle), np.sin(angle)
    first = np.arange(128)[None, None, :] < 64
    unit0 = np.arange(UNITS)[:, None, None] == 0
    sign = np.where(first, 1.0, -1.0)
    rr = np.where(unit0, np.where(first, c, 0.0), c)
    ri = np.where(unit0, np.where(first, -s, 0.0), -s)
    ir = np.where(unit0, np.where(first, 0.0, c), sign * s)
    ii = np.where(unit0, np.where(first, 0.0, -s), sign * c)
    top = np.concatenate([rr, ri], axis=2)
    bottom = np.concatenate([ir, ii], axis=2)
    return np.concatenate([top, bottom], axis=1).astype(jnp.bfloat16)


def lag_table():
    bins = unit_bins()[:, :, None].astype(np.int64)
    tau = np.arange(LAGS)[None, None, :] - LAGS // 2
    angle = 2.0 * np.pi * ((bins * tau) % SAMP) / SAMP
    return (np.concatenate([np.cos(angle), -np.sin(angle)], axis=1) / 256.0).astype(jnp.bfloat16)


def real_dft(values):
    n = len(values)
    if n == 1:
        return [values[0]], [None]
    if n == 2:
        return [values[0] + values[1], values[0] - values[1]], [None, None]
    er, ei = real_dft(values[0::2])
    odr, odi = real_dft(values[1::2])
    half, quarter = n // 2, n // 4
    re, im = [None] * (half + 1), [None] * (half + 1)
    re[0], re[half] = er[0] + odr[0], er[0] - odr[0]
    re[quarter], im[quarter] = er[quarter], -odr[quarter]
    for k in range(1, quarter):
        c, s = math.cos(2 * math.pi * k / n), math.sin(2 * math.pi * k / n)
        if 8 * k == n:
            pr, pi = (odr[k] + odi[k]) * c, (odi[k] - odr[k]) * c
        else:
            pr, pi = odr[k] * c + odi[k] * s, odi[k] * c - odr[k] * s
        re[k], im[k] = er[k] + pr, ei[k] + pi
        re[half - k], im[half - k] = er[k] - pr, pi - ei[k]
    return re, im


def kernel(
    rows, traces_hbm, alive_ref, pair_ref, window_ref, table_hbm, lag_hbm, out_ref,
    x, mid, spec, level, table, w,
    both, lag, idx, first_pick, second_pick, total, half_out, half_in, piece, got,
    y_send, y_recv, x_send, x_recv, idx_send, idx_recv, half_send, half_recv, sum_send, sum_recv, local,
):
    me, seg = lax.axis_index("chan"), lax.axis_index("seg")
    row, y = me // ROW, me % ROW
    zh, core = seg // 2, seg % 2
    before, after = (row + rows - 1) % rows, (row + 1) % rows
    mine = y * 2 + zh

    def at(r, q):
        return (r * ROW + q // 2, (q % 2) * 2 + core)

    def remote(src, dst, send, recv, device):
        return pltpu.make_async_remote_copy(
            src_ref=src, dst_ref=dst, send_sem=send, recv_sem=recv, device_id=device, device_id_type=MESH
        )

    sibling = (me, zh * 2 + 1 - core)
    barrier = pltpu.get_barrier_semaphore()

    def greet(device):
        pl.semaphore_signal(barrier, inc=1, device_id=device, device_id_type=MESH)

    load = [
        pltpu.make_async_copy(traces_hbm.at[pl.ds(16 * h, 16)], x.at[pl.ds(16 * h, 16)], local.at[h]) for h in range(2)
    ]
    load[0].start()
    fetch_table = pltpu.make_async_copy(table_hbm, table, local.at[2])
    fetch_table.start()
    load[1].start()
    fetch_lag = pltpu.make_async_copy(lag_hbm.at[pl.ds(8 * y, 8)], lag, local.at[3])
    fetch_lag.start()

    greet(sibling)
    for k in range(8):
        if k:
            greet(at(row, (mine + k) % 8))
        greet(at(before, (mine + k) % 8))
        greet(at(after, (mine + k) % 8))

    def keep_own(h):
        return pltpu.make_async_copy(w.at[h, y], both.at[0, h, :, :, y], local.at[4 + h])

    def column(values):
        n = values.shape[1]
        diagonal = lax.broadcasted_iota(jnp.int32, (n, n), 0) == lax.broadcasted_iota(jnp.int32, (n, n), 1)
        return jnp.sum(jnp.where(diagonal, values.astype(jnp.float32), 0.0), axis=1, keepdims=True)

    live = column(alive_ref[...])

    def whiten(h):
        load[h].wait()

        def first_stage(block, carry):
            channels = pl.ds(16 * h + 2 * block, 2)
            values = [
                x[channels, :, pl.ds(128 * t, 128)].astype(jnp.float32).reshape(8, 128) for t in range(64)
            ]
            re, im = real_dft(values)
            at_rows = pl.ds(pl.multiple_of(8 * block, 8), 8)
            mid[0, at_rows, 0:128] = re[0]
            mid[0, at_rows, 128:256] = re[32]
            for k in range(1, 32):
                mid[k, at_rows, 0:128] = re[k]
                mid[k, at_rows, 128:256] = im[k]
            return carry

        lax.fori_loop(0, 8, first_stage, 0)
        if h == 0:
            fetch_table.wait()
        level[...] = jnp.zeros_like(level)

        def second_stage(u, carry):
            result = jnp.dot(mid[u].astype(jnp.bfloat16), table[u], preferred_element_type=jnp.float32)
            re, im = result[:, :128], result[:, 128:]
            spec[u, 0] = re
            spec[u, 1] = im
            level[...] += jnp.sqrt(re * re + im * im)
            return carry

        lax.fori_loop(0, UNITS, second_stage, 0, unroll=4)
        sums = level[...]
        level[...] = 1.0 / ((sums + pltpu.roll(sums, 64, 1)) * (1.0 / BAND) + EPS)
        scales = [level[pl.ds(s, 16, stride=SEG), :] * live[16 * h : 16 * h + 16] for s in range(SEG)]

        def third_stage(u, carry):
            for s in range(SEG):
                for part in range(2):
                    value = spec[u, part, pl.ds(s, 16, stride=SEG), :] * scales[s]
                    w[h, u // 8, u % 8, s, :, pl.ds(128 * part, 128)] = value.astype(jnp.bfloat16)
            return carry

        lax.fori_loop(0, UNITS, third_stage, 0, unroll=2)

    def y_copy(d, h, u):
        to = (y + d) % ROW
        return remote(
            w.at[h, to, u], both.at[0, h, u, :, y], y_send.at[d - 1, h, u], y_recv.at[d - 1, h, u], (row * ROW + to, seg)
        )

    def y_arrival(d, h, u):
        source = (y + ROW - d) % ROW
        return remote(
            w.at[h, y, u], both.at[0, h, u, :, source], y_send.at[d - 1, h, u], y_recv.at[d - 1, h, u],
            (row * ROW + source, seg),
        )

    def x_copy(h, u):
        to = (row + rows - 1 + 2 * (u // 4)) % rows
        return remote(both.at[0, h, u], both.at[1, h, u], x_send.at[h, u], x_recv.at[h, u], (to * ROW + y, seg))

    def unit_of(step):
        return (step % 2) * 4 + (step % 8) // 2

    def start_y(step):
        for d in (2, 1, 3):
            y_copy(d, step // 8, unit_of(step)).start()

    own_idx = pltpu.make_async_copy(pair_ref, idx.at[y], local.at[6])
    own_idx.start()

    def idx_copy(k, slot):
        r = row if k < ROW else after
        return remote(pair_ref, idx.at[slot], idx_send.at[k], idx_recv.at[k], (r * ROW + (y + k) % ROW, seg))

    whiten(0)
    pl.semaphore_wait(barrier, 24)
    for step in range(AHEAD):
        start_y(step)
    for k in range(1, 8):
        idx_copy(k, y + (0 if k < ROW else ROW)).start()
    keep_own(0).start()
    whiten(1)
    keep_own(1).start()
    total[...] = jnp.zeros_like(total)

    channel_row = lax.broadcasted_iota(jnp.int32, (128, 128), 0)
    channel = ((channel_row // 16) % ROW) * CH + (channel_row // 64) * 16 + channel_row % 16

    def make_picks(slot, carry):
        side = slot // ROW
        base = jnp.where(side == 0, row, before) * (ROW * CH)
        at_rows = pl.ds(pl.multiple_of((slot % ROW) * 128, 128), 128)

        def picks(which, shift):
            hit = channel + (base + shift) == idx[slot, which : which + 1, :]
            return jnp.where(hit, 1.0, 0.0).T.astype(jnp.bfloat16)

        first_pick[side, at_rows, :] = picks(0, 0)
        second_pick[side, at_rows, 0:128] = picks(1, 0)
        second_pick[side, at_rows, 128:256] = picks(1, 128)
        return carry

    def spectra(side, u, s):
        return [both[side, h, u, s].reshape(64, 256) for h in range(2)]

    def correlate(u):
        late = u // 4
        cross_re = cross_im = None
        for s in range(SEG):
            near = jnp.concatenate(spectra(late, u, s), axis=0)
            far = jnp.concatenate(spectra(1 - late, u, s), axis=0)
            a = jnp.dot(first_pick[late], near, preferred_element_type=jnp.float32)
            b = jnp.dot(
                second_pick[late], jnp.concatenate([near, far], axis=0), preferred_element_type=jnp.float32
            )
            ar, ai, br, bi = a[:, :128], a[:, 128:], b[:, :128], b[:, 128:]
            re, im = ar * br + ai * bi, ai * br - ar * bi
            cross_re = re if cross_re is None else cross_re + re
            cross_im = im if cross_im is None else cross_im + im
        cross = jnp.concatenate([cross_re, cross_im], axis=1).astype(jnp.bfloat16)
        total[late] += jnp.dot(cross, lag[u], preferred_element_type=jnp.float32)

    def advance(step, carry):
        @pl.when(step + AHEAD < 16)
        def _():
            start_y(step + AHEAD)

        @pl.when(step % 8 == 0)
        def _():
            @pl.when(step == 0)
            def _():
                keep_own(0).wait()

            @pl.when(step == 8)
            def _():
                keep_own(1).wait()

        @pl.when(step < 16)
        def _():
            h, u = step // 8, unit_of(step)
            for d in (1, 3, 2):
                y_arrival(d, h, u).wait_recv()
            x_copy(h, u).start()

        @pl.when(step == PICKS)
        def _():
            own_idx.wait()
            for k in range(1, 8):
                idx_copy(k, (y + ROW - k % ROW) % ROW + (0 if k < ROW else ROW)).wait_recv()
            lax.fori_loop(0, 8, make_picks, 0)
            fetch_lag.wait()

        @pl.when(step >= 8 + DELAY)
        def _():
            u = unit_of(step - DELAY)
            for h in range(2):
                x_copy(h, u).wait_recv()
            correlate(u)

        return carry

    lax.fori_loop(0, 16 + DELAY, advance, 0)

    def rows_of(q, c):
        return pl.ds(pl.multiple_of(q * 64 + c * 32, 32), 32)

    def half_copy(side):
        return remote(half_out.at[side], half_in.at[side], half_send.at[side], half_recv.at[side], sibling)

    for side in range(2):
        def pack(q, carry, side=side):
            half_out[side, q] = total[side, rows_of(q, 1 - core), :].astype(jnp.bfloat16)
            return carry

        lax.fori_loop(0, 8, pack, 0)
        half_copy(side).start()

    def sum_copy(side, k):
        to = row if side == 0 else before
        q = (mine + k) % 8
        return remote(piece.at[side, q], got.at[side, k], sum_send.at[side, k], sum_recv.at[side, k], at(to, q))

    for side in range(2):
        half_copy(side).wait_recv()

        def combine(q, carry, side=side):
            value = total[side, rows_of(q, core), :] + half_in[side, q].astype(jnp.float32)
            piece[side, q] = value.astype(jnp.bfloat16)
            return carry

        lax.fori_loop(0, 8, combine, 0)
        for k in range(1 - side, 8):
            sum_copy(side, k).start()

    def sent(u, carry):
        for h in range(2):
            for d in (1, 2, 3):
                y_copy(d, h, u).wait_send()
            x_copy(h, u).wait_send()
        return carry

    lax.fori_loop(0, 8, sent, 0)
    for k in range(1, 8):
        idx_copy(k, y + (0 if k < ROW else ROW)).wait_send()
    for side in range(2):
        half_copy(side).wait_send()

    result = piece[0, mine].astype(jnp.float32)
    for side in range(2):
        for k in range(1 - side, 8):
            sum_copy(side, k).wait_recv()
            result = result + got[side, k].astype(jnp.float32)
    widest = column(window_ref[...])
    lags = jnp.abs(lax.broadcasted_iota(jnp.int32, (32, LAGS), 1) - LAGS // 2).astype(jnp.float32)
    out_ref[...] = jnp.where(lags <= widest, result, 0.0)
    for side in range(2):
        for k in range(1 - side, 8):
            sum_copy(side, k).wait_send()


def body(traces, alive, pair_chan, lag_window):
    rows = lax.axis_size("chan") // ROW
    dma = pltpu.SemaphoreType.DMA
    vmem = pl.BlockSpec(memory_space=pltpu.VMEM)
    hbm = pl.BlockSpec(memory_space=pl.ANY)
    pieces = pltpu.VMEM((2, 8, 32, LAGS), jnp.bfloat16)
    return pl.pallas_call(
        functools.partial(kernel, rows),
        out_shape=jax.ShapeDtypeStruct((32, LAGS), jnp.float32),
        in_specs=[hbm, vmem, vmem, vmem, hbm, hbm],
        out_specs=vmem,
        scratch_shapes=[
            pltpu.VMEM((CH, SEG, SAMP), jnp.bfloat16),
            pltpu.VMEM((UNITS, 64, 256), jnp.float32),
            pltpu.VMEM((UNITS, 2, 64, 128), jnp.float32),
            pltpu.VMEM((64, 128), jnp.float32),
            pltpu.VMEM((UNITS, 256, 256), jnp.bfloat16),
            pltpu.VMEM((2, ROW, 8, SEG, 16, 256), jnp.bfloat16),
            pltpu.VMEM((2, 2, 8, SEG, ROW, 16, 256), jnp.bfloat16),
            pltpu.VMEM((8, 256, LAGS), jnp.bfloat16),
            pltpu.VMEM((8, 2, 128), jnp.int32),
            pltpu.VMEM((2, 512, 128), jnp.bfloat16),
            pltpu.VMEM((2, 512, 256), jnp.bfloat16),
            pltpu.VMEM((2, 512, LAGS), jnp.float32),
            pieces,
            pieces,
            pieces,
            pieces,
            dma((3, 2, 8)),
            dma((3, 2, 8)),
            dma((2, 8)),
            dma((2, 8)),
            dma((8,)),
            dma((8,)),
            dma((2,)),
            dma((2,)),
            dma((2, 8)),
            dma((2, 8)),
            dma((7,)),
        ],
        compiler_params=pltpu.CompilerParams(
            collective_id=0, has_side_effects=True, vmem_limit_bytes=48 * 2**20
        ),
    )(
        traces,
        alive[None],
        pair_chan.T,
        lag_window[None],
        jnp.asarray(second_table()),
        jnp.asarray(lag_table()),
    )


def solution(mesh):
    in_specs = (P("chan", "seg", None), P("chan"), P("chan", None), P(("chan", "seg")))
    out_specs = P(("chan", "seg"), None)
    return jax.shard_map(body, mesh=mesh, in_specs=in_specs, out_specs=out_specs, check_vma=False)
```

time: 66.2 us -> 58.1 us (0.88)
  Pallas kernels: 62 us -> 53.7 us
  local copies, waits for them, and re-layouts: 3.25 us -> 4.21 us
    pallas_call x2 -> x1, Pallas kernels: 62 us -> 53.7 us  [body(): pl.pallas_call(functools.partial(kernel, rows), out_shape=jax.ShapeDtypeS...]
    unnamed x5 -> x9, local copies, waits for them, and re-layouts: 0.64 us -> 4.21 us
    reshape x1 -> x0, local copies, waits for them, and re-layouts: 2.54 us -> none  [body(): traces.reshape(CH * SEG, SAMP)]
where the time goes in v3:
time: 58.1 us; the launch traced here: 57.9 us
  Pallas kernels  53.7 us (92%)
  local copies, waits for them, and re-layouts  4.21 us (7%)
    pallas_call x1, Pallas kernels, body(): pl.pallas_call(functools.partial(kernel, rows), out_shape=jax.ShapeDtypeS...  53.7 us
    unnamed x9, local copies, waits for them, and re-layouts  4.21 us

profile of v3, /device:TPU:1, one launch (start us, length us, event | category | flops | bytes accessed | tf_op | source)
XLA Modules:
  0.0 57.9 jit_solution(6631570445472611427)
XLA Ops:
  0.0 0.0 copy-start
  0.0 1.6 %copy-done = bf16[32,4,8192]{2,1,0:T(4,128)(2,1)S(1)} copy-done((bf16[32,4,8192]{2,1,0:T(4,128)(2,1)S(1)}, bf16[32,4,8192]{2,1,0:T(4,128)(2,1)}, u32[]{:S(2)}) %copy-start) | copy-done | bytes 2097176
  1.6 0.0 copy-start.1
  1.6 0.7 %copy-done.1 = s32[128,2]{0,1:T(2,128)S(1)} copy-done((s32[128,2]{0,1:T(2,128)S(1)}, s32[128,2]{0,1:T(2,128)}, u32[]{:S(2)}) %copy-start.1) | copy-done | bytes 1048
  2.3 0.0 copy-start.2
  2.3 0.7 %copy-done.2 = s32[32]{0:T(128)S(1)} copy-done((s32[32]{0:T(128)S(1)}, s32[32]{0:T(128)}, u32[]{:S(2)}) %copy-start.2) | copy-done | bytes 152
  2.9 0.0 copy-start.3
  2.9 0.7 %copy-done.3 = s32[32]{0:T(128)S(1)} copy-done((s32[32]{0:T(128)S(1)}, s32[32]{0:T(128)}, u32[]{:S(2)}) %copy-start.3) | copy-done | bytes 152
  3.6 53.7 %shard_map.64 = f32[32,512]{1,0:T(8,128)S(1)} custom-call(bf16[32,4,8192]{2,1,0:T(4,128)(2,1)S(1)} %copy-done, s32[1,32]{1,0:T(1,128)S(1)} %bitcast.4, s32[2,128]{1,0:T(2,128)S(1)} %bitcast.3, s32[1,32]{1,0:T(1,128)S(1)} %bitcast.5, bf16[32,256,256]{2,1,0:T(8,128)(2,1)} %constant.4.clone.table_hbm, bf16[32,256,512]{2,1,0:T(8,128)(2,1)} %constant.5.clone.lag_hbm), custom_call_target="tpu_custom_call" | custom-call | tf_op jit(solution)/shard_map/pallas_call | solution.py:361
  57.3 0.6 %copy.8 = f32[32,512]{1,0:T(8,128)} copy(f32[32,512]{1,0:T(8,128)S(1)} %shard_map.64) | data formatting | bytes 131072
Async XLA Ops:
  0.0 1.6 %copy-start = (bf16[32,4,8192]{2,1,0:T(4,128)(2,1)S(1)}, bf16[32,4,8192]{2,1,0:T(4,128)(2,1)}, u32[]{:S(2)}) copy-start(bf16[32,4,8192]{2,1,0:T(4,128)(2,1)} %traces_hbm.1) | copy-start | bytes 6291460
  1.6 0.7 %copy-start.1 = (s32[128,2]{0,1:T(2,128)S(1)}, s32[128,2]{0,1:T(2,128)}, u32[]{:S(2)}) copy-start(s32[128,2]{0,1:T(2,128)} %param.8) | copy-start | bytes 3076
  2.3 0.7 %copy-start.2 = (s32[32]{0:T(128)S(1)}, s32[32]{0:T(128)}, u32[]{:S(2)}) copy-start(s32[32]{0:T(128)} %param.7) | copy-start | bytes 388
  2.9 0.7 %copy-start.3 = (s32[32]{0:T(128)S(1)}, s32[32]{0:T(128)}, u32[]{:S(2)}) copy-start(s32[32]{0:T(128)} %param.9) | copy-start | bytes 388

commit v4 on v3

v4 whole, which is shorter than its diff:
```python
import functools
import math

import jax
import jax.numpy as jnp
import numpy as np
from jax import lax
from jax.experimental import pallas as pl
from jax.experimental.pallas import tpu as pltpu
from jax.sharding import PartitionSpec as P

FREQ = 4096
SAMP = 8192
BAND = 64
LAGS = 512
UNITS = 32
ROW = 4
CH = 32
SEG = 4
EPS = 1e-06
AHEAD = 3
DELAY = 2
PICKS = 4
MESH = pl.DeviceIdType.MESH


def unit_bins():
    u = np.arange(UNITS)[:, None]
    lane = np.arange(128)[None, :]
    low = np.where(lane < 64, u, np.where(u == 0, 32, 64 - u))
    return low + 64 * (lane % 64)


def second_table():
    bins = unit_bins()[:, None, :]
    t2 = np.arange(128)[None, :, None]
    angle = 2.0 * np.pi * ((t2 * bins) % SAMP) / SAMP
    c, s = np.cos(angle), np.sin(angle)
    first = np.arange(128)[None, None, :] < 64
    unit0 = np.arange(UNITS)[:, None, None] == 0
    sign = np.where(first, 1.0, -1.0)
    rr = np.where(unit0, np.where(first, c, 0.0), c)
    ri = np.where(unit0, np.where(first, -s, 0.0), -s)
    ir = np.where(unit0, np.where(first, 0.0, c), sign * s)
    ii = np.where(unit0, np.where(first, 0.0, -s), sign * c)
    top = np.concatenate([rr, ri], axis=2)
    bottom = np.concatenate([ir, ii], axis=2)
    return np.concatenate([top, bottom], axis=1).astype(jnp.bfloat16)


def lag_table():
    bins = unit_bins()[:, :, None].astype(np.int64)
    tau = np.arange(LAGS)[None, None, :] - LAGS // 2
    angle = 2.0 * np.pi * ((bins * tau) % SAMP) / SAMP
    return (np.concatenate([np.cos(angle), -np.sin(angle)], axis=1) / 256.0).astype(jnp.bfloat16)


def real_dft(values):
    n = len(values)
    if n == 1:
        return [values[0]], [None]
    if n == 2:
        return [values[0] + values[1], values[0] - values[1]], [None, None]
    er, ei = real_dft(values[0::2])
    odr, odi = real_dft(values[1::2])
    half, quarter = n // 2, n // 4
    re, im = [None] * (half + 1), [None] * (half + 1)
    re[0], re[half] = er[0] + odr[0], er[0] - odr[0]
    re[quarter], im[quarter] = er[quarter], -odr[quarter]
    for k in range(1, quarter):
        c, s = math.cos(2 * math.pi * k / n), math.sin(2 * math.pi * k / n)
        if 8 * k == n:
            pr, pi = (odr[k] + odi[k]) * c, (odi[k] - odr[k]) * c
        else:
            pr, pi = odr[k] * c + odi[k] * s, odi[k] * c - odr[k] * s
        re[k], im[k] = er[k] + pr, ei[k] + pi
        re[half - k], im[half - k] = er[k] - pr, pi - ei[k]
    return re, im


def kernel(
    rows, traces_hbm, alive_hbm, pair_hbm, window_hbm, table_hbm, lag_hbm, out_ref,
    alive_ref, pair_ref, window_ref, x, mid, spec, level, table, w,
    both, lag, idx, first_pick, second_pick, total, piece, got,
    y_send, y_recv, own_send, own_recv, x_send, x_recv, rest_send, rest_recv,
    idx_send, idx_recv, sum_send, sum_recv, local,
):
    me, seg = lax.axis_index("chan"), lax.axis_index("seg")
    row, y = me // ROW, me % ROW
    zh, core = seg // 2, seg % 2
    before, after = (row + rows - 1) % rows, (row + 1) % rows
    mine = y * 2 + zh
    pair_row = (row + rows - core) % rows
    my_segs = pl.ds(SEG * core, SEG)

    def at(r, q, c):
        return (r * ROW + q // 2, (q % 2) * 2 + c)

    def remote(src, dst, send, recv, device):
        return pltpu.make_async_remote_copy(
            src_ref=src, dst_ref=dst, send_sem=send, recv_sem=recv, device_id=device, device_id_type=MESH
        )

    sibling = (me, zh * 2 + 1 - core)
    barrier = pltpu.get_barrier_semaphore()

    def greet(device):
        pl.semaphore_signal(barrier, inc=1, device_id=device, device_id_type=MESH)

    load = [
        pltpu.make_async_copy(traces_hbm.at[pl.ds(16 * h, 16)], x.at[pl.ds(16 * h, 16)], local.at[h]) for h in range(2)
    ]
    small = [
        pltpu.make_async_copy(src, dst, local.at[7 + k])
        for k, (src, dst) in enumerate(((alive_hbm, alive_ref), (pair_hbm, pair_ref), (window_hbm, window_ref)))
    ]
    load[0].start()
    for copy in small:
        copy.start()
    fetch_table = pltpu.make_async_copy(table_hbm, table, local.at[2])
    fetch_table.start()
    load[1].start()
    fetch_lag = pltpu.make_async_copy(lag_hbm.at[pl.ds(8 * y + 4 * core, 4)], lag, local.at[3])
    fetch_lag.start()

    greet(sibling)
    for k in range(8):
        for c in range(2):
            if k:
                greet(at(row, (mine + k) % 8, c))
            greet(at(before, (mine + k) % 8, c))
            greet(at(after, (mine + k) % 8, c))

    def column(values):
        n = values.shape[1]
        diagonal = lax.broadcasted_iota(jnp.int32, (n, n), 0) == lax.broadcasted_iota(jnp.int32, (n, n), 1)
        return jnp.sum(jnp.where(diagonal, values.astype(jnp.float32), 0.0), axis=1, keepdims=True)

    for copy in small:
        copy.wait()
    live = column(alive_ref[...])

    def whiten(h):
        load[h].wait()

        def first_stage(block, carry):
            channels = pl.ds(16 * h + 2 * block, 2)
            values = [
                x[channels, :, pl.ds(128 * t, 128)].astype(jnp.float32).reshape(8, 128) for t in range(64)
            ]
            re, im = real_dft(values)
            at_rows = pl.ds(pl.multiple_of(8 * block, 8), 8)
            mid[0, at_rows, 0:128] = re[0]
            mid[0, at_rows, 128:256] = re[32]
            for k in range(1, 32):
                mid[k, at_rows, 0:128] = re[k]
                mid[k, at_rows, 128:256] = im[k]
            return carry

        lax.fori_loop(0, 8, first_stage, 0)
        if h == 0:
            fetch_table.wait()
        level[...] = jnp.zeros_like(level)

        def second_stage(u, carry):
            result = jnp.dot(mid[u].astype(jnp.bfloat16), table[u], preferred_element_type=jnp.float32)
            re, im = result[:, :128], result[:, 128:]
            spec[u, 0] = re
            spec[u, 1] = im
            level[...] += jnp.sqrt(re * re + im * im)
            return carry

        lax.fori_loop(0, UNITS, second_stage, 0, unroll=4)
        sums = level[...]
        level[...] = 1.0 / ((sums + pltpu.roll(sums, 64, 1)) * (1.0 / BAND) + EPS)
        scales = [level[pl.ds(s, 16, stride=SEG), :] * live[16 * h : 16 * h + 16] for s in range(SEG)]

        def third_stage(u, carry):
            for s in range(SEG):
                for part in range(2):
                    value = spec[u, part, pl.ds(s, 16, stride=SEG), :] * scales[s]
                    w[h, u // 8, u % 8, s, :, pl.ds(128 * part, 128)] = value.astype(jnp.bfloat16)
            return carry

        lax.fori_loop(0, UNITS, third_stage, 0, unroll=2)

    def keep_own(h):
        return pltpu.make_async_copy(
            w.at[h, y, pl.ds(4 * core, 4)], both.at[0, h, :, my_segs, 0], local.at[4 + h]
        )

    def give_own(h):
        return remote(
            w.at[h, y, pl.ds(4 * (1 - core), 4)], both.at[0, h, :, my_segs, 0], own_send.at[h], own_recv.at[h], sibling
        )

    def take_own(h):
        other = pl.ds(SEG * (1 - core), SEG)
        return remote(w.at[h, y, pl.ds(0, 4)], both.at[0, h, :, other, 0], own_send.at[h], own_recv.at[h], sibling)

    def y_copy(d, h, u, side):
        to = (y + d) % ROW
        return remote(
            w.at[h, to, 4 * side + u], both.at[0, h, u, my_segs, d], y_send.at[side, d - 1, h, u],
            y_recv.at[core, d - 1, h, u], (row * ROW + to, zh * 2 + side),
        )

    def y_arrival(d, h, u, c):
        return remote(
            w.at[h, y, u], both.at[0, h, u, pl.ds(SEG * c, SEG), d], y_send.at[0, d - 1, h, u],
            y_recv.at[c, d - 1, h, u], sibling,
        )

    def x_copy(h, u, side):
        to = before if side == 0 else after
        return remote(
            w.at[h, y, 4 * side + u], both.at[1, h, u, my_segs, 0], x_send.at[side, h, u], x_recv.at[core, h, u],
            (to * ROW + y, zh * 2 + side),
        )

    def x_arrival(h, u, c):
        return remote(
            w.at[h, y, u], both.at[1, h, u, pl.ds(SEG * c, SEG), 0], x_send.at[0, h, u], x_recv.at[c, h, u], sibling
        )

    def rest_copy(h, u):
        to = (row + rows - 1 + 2 * core) % rows
        others = pl.ds(1, 3)
        return remote(
            both.at[0, h, u, :, others], both.at[1, h, u, :, others], rest_send.at[h, u], rest_recv.at[h, u],
            (to * ROW + y, seg),
        )

    def start_y(step):
        h, u = step // 4, step % 4
        for d in (2, 1, 3):
            for side in range(2):
                y_copy(d, h, u, side).start()
        for side in range(2):
            x_copy(h, u, side).start()

    def idx_copy(k, slot):
        r = (row + core) % rows
        return remote(pair_ref, idx.at[slot], idx_send.at[k], idx_recv.at[k], (r * ROW + (y + k) % ROW, seg))

    own_idx = pltpu.make_async_copy(pair_ref, idx.at[y], local.at[6])

    whiten(0)
    pl.semaphore_wait(barrier, 47)
    for step in range(AHEAD):
        start_y(step)
    for k in range(1, ROW):
        idx_copy(k, y).start()

    @pl.when(core == 0)
    def _():
        own_idx.start()

    @pl.when(core == 1)
    def _():
        idx_copy(0, y).start()

    give_own(0).start()
    keep_own(0).start()
    whiten(1)
    give_own(1).start()
    keep_own(1).start()
    total[...] = jnp.zeros_like(total)

    channel_row = lax.broadcasted_iota(jnp.int32, (128, 128), 0)
    source_y = (y + ROW - (channel_row // 16) % ROW) % ROW
    channel = pair_row * (ROW * CH) + source_y * CH + (channel_row // 64) * 16 + channel_row % 16

    def make_picks(slot, carry):
        at_rows = pl.ds(pl.multiple_of(slot * 128, 128), 128)

        def picks(which, shift):
            hit = channel + shift == idx[slot, which : which + 1, :]
            return jnp.where(hit, 1.0, 0.0).T.astype(jnp.bfloat16)

        first_pick[at_rows, :] = picks(0, 0)
        second_pick[at_rows, 0:128] = picks(1, 0)
        second_pick[at_rows, 128:256] = picks(1, 128)
        return carry

    def spectra(side, u, s):
        return [both[side, h, u, s].reshape(64, 256) for h in range(2)]

    def correlate(u):
        cross_re = cross_im = None
        for s in range(2 * SEG):
            near = jnp.concatenate(spectra(core, u, s), axis=0)
            far = jnp.concatenate(spectra(1 - core, u, s), axis=0)
            a = jnp.dot(first_pick[...], near, preferred_element_type=jnp.float32)
            b = jnp.dot(second_pick[...], jnp.concatenate([near, far], axis=0), preferred_element_type=jnp.float32)
            ar, ai, br, bi = a[:, :128], a[:, 128:], b[:, :128], b[:, 128:]
            re, im = ar * br + ai * bi, ai * br - ar * bi
            cross_re = re if cross_re is None else cross_re + re
            cross_im = im if cross_im is None else cross_im + im
        cross = jnp.concatenate([cross_re, cross_im], axis=1).astype(jnp.bfloat16)
        total[...] += jnp.dot(cross, lag[u], preferred_element_type=jnp.float32)

    def advance(step, carry):
        @pl.when(step + AHEAD < 8)
        def _():
            start_y(step + AHEAD)

        @pl.when(step < 8)
        def _():
            h, u = step // 4, step % 4
            for d in (1, 3, 2):
                for c in range(2):
                    y_arrival(d, h, u, c).wait_recv()
            rest_copy(h, u).start()

        @pl.when(step == PICKS)
        def _():
            @pl.when(core == 0)
            def _():
                own_idx.wait()

            @pl.when(core == 1)
            def _():
                idx_copy(0, y).wait_recv()

            for k in range(1, ROW):
                idx_copy(k, (y + ROW - k) % ROW).wait_recv()
            lax.fori_loop(0, ROW, make_picks, 0)
            fetch_lag.wait()
            for h in range(2):
                keep_own(h).wait()
                take_own(h).wait_recv()

        @pl.when(step >= 4 + DELAY)
        def _():
            u = (step - DELAY) % 4
            for h in range(2):
                for c in range(2):
                    x_arrival(h, u, c).wait_recv()
                rest_copy(h, u).wait_recv()
            correlate(u)

        return carry

    lax.fori_loop(0, 8 + DELAY, advance, 0)

    def sum_copy(k, c):
        q = (mine + k) % 8
        return remote(piece.at[q, c], got.at[core, k], sum_send.at[k, c], sum_recv.at[core, k], at(pair_row, q, c))

    def sum_arrival(side, k):
        return remote(piece.at[0, 0], got.at[side, k], sum_send.at[k, 0], sum_recv.at[side, k], sibling)

    for k in (4, 5, 3, 7, 1, 6, 2, 0):
        q = (mine + k) % 8
        for c in range(2):
            piece[q, c] = total[pl.ds(pl.multiple_of(q * 64 + c * 32, 32), 32), :].astype(jnp.bfloat16)
            if k or c:
                sum_copy(k, c).start()
    stays = core == 0

    @pl.when(stays)
    def _():
        got[0, 0] = piece[mine, 0]

    @pl.when(core == 1)
    def _():
        sum_copy(0, 0).start()

    def sent(u, carry):
        for h in range(2):
            for side in range(2):
                for d in (1, 2, 3):
                    y_copy(d, h, u, side).wait_send()
                x_copy(h, u, side).wait_send()
            rest_copy(h, u).wait_send()
        return carry

    lax.fori_loop(0, 4, sent, 0)
    for h in range(2):
        give_own(h).wait_send()
    for k in range(1, ROW):
        idx_copy(k, y).wait_send()

    @pl.when(core == 1)
    def _():
        idx_copy(0, y).wait_send()
        sum_arrival(0, 0).wait_recv()

    widest = column(window_ref[...])
    lags = jnp.abs(lax.broadcasted_iota(jnp.int32, (32, LAGS), 1) - LAGS // 2).astype(jnp.float32)
    for side, k in [(0, k) for k in range(1, 8)] + [(1, k) for k in range(8)]:
        sum_arrival(side, k).wait_recv()
    result = jnp.zeros((32, LAGS), jnp.float32)
    for side in range(2):
        for k in range(8):
            result = result + got[side, k].astype(jnp.float32)
    out_ref[...] = jnp.where(lags <= widest, result, 0.0)
    for k in range(8):
        for c in range(2):
            if k or c:
                sum_copy(k, c).wait_send()

    @pl.when(core == 1)
    def _():
        sum_copy(0, 0).wait_send()


def body(traces, alive, pair_chan, lag_window):
    rows = lax.axis_size("chan") // ROW
    dma = pltpu.SemaphoreType.DMA
    hbm = pl.BlockSpec(memory_space=pl.ANY)
    return pl.pallas_call(
        functools.partial(kernel, rows),
        out_shape=jax.ShapeDtypeStruct((32, LAGS), jnp.float32),
        in_specs=[hbm] * 6,
        out_specs=pl.BlockSpec(memory_space=pltpu.VMEM),
        scratch_shapes=[
            pltpu.VMEM((1, CH), jnp.int32),
            pltpu.VMEM((2, 128), jnp.int32),
            pltpu.VMEM((1, 32), jnp.int32),
            pltpu.VMEM((CH, SEG, SAMP), jnp.bfloat16),
            pltpu.VMEM((UNITS, 64, 256), jnp.float32),
            pltpu.VMEM((UNITS, 2, 64, 128), jnp.float32),
            pltpu.VMEM((64, 128), jnp.float32),
            pltpu.VMEM((UNITS, 256, 256), jnp.bfloat16),
            pltpu.VMEM((2, ROW, 8, SEG, 16, 256), jnp.bfloat16),
            pltpu.VMEM((2, 2, 4, 2 * SEG, ROW, 16, 256), jnp.bfloat16),
            pltpu.VMEM((4, 256, LAGS), jnp.bfloat16),
            pltpu.VMEM((ROW, 2, 128), jnp.int32),
            pltpu.VMEM((512, 128), jnp.bfloat16),
            pltpu.VMEM((512, 256), jnp.bfloat16),
            pltpu.VMEM((512, LAGS), jnp.float32),
            pltpu.VMEM((8, 2, 32, LAGS), jnp.bfloat16),
            pltpu.VMEM((2, 8, 32, LAGS), jnp.bfloat16),
            dma((2, 3, 2, 4)),
            dma((2, 3, 2, 4)),
            dma((2,)),
            dma((2,)),
            dma((2, 2, 4)),
            dma((2, 2, 4)),
            dma((2, 4)),
            dma((2, 4)),
            dma((ROW,)),
            dma((ROW,)),
            dma((8, 2)),
            dma((2, 8)),
            dma((10,)),
        ],
        compiler_params=pltpu.CompilerParams(
            collective_id=0, has_side_effects=True, vmem_limit_bytes=60 * 2**20
        ),
    )(
        traces,
        alive[None],
        pair_chan.T,
        lag_window[None],
        jnp.asarray(second_table()),
        jnp.asarray(lag_table()),
    )


def solution(mesh):
    in_specs = (P("chan", "seg", None), P("chan"), P("chan", None), P(("chan", "seg")))
    out_specs = P(("chan", "seg"), None)
    return jax.shard_map(body, mesh=mesh, in_specs=in_specs, out_specs=out_specs, check_vma=False)
```

time: 58.1 us -> 53.8 us (0.926)
  local copies, waits for them, and re-layouts: 4.21 us -> 1.47 us
  Pallas kernels: 53.7 us -> 52.1 us
    unnamed x9 -> x1, local copies, waits for them, and re-layouts: 4.21 us -> 1.47 us
    pallas_call x1, Pallas kernels: 53.7 us -> 52.1 us  [body(): pl.pallas_call(functools.partial(kernel, rows), out_shape=jax.ShapeDtypeS...]
where the time goes in v4:
time: 53.8 us; the launch traced here: 53.6 us
  Pallas kernels  52.1 us (97%)
  local copies, waits for them, and re-layouts  1.47 us (3%)
    pallas_call x1, Pallas kernels, body(): pl.pallas_call(functools.partial(kernel, rows), out_shape=jax.ShapeDtypeS...  52.1 us
    unnamed x1, local copies, waits for them, and re-layouts  1.47 us

profile of v4, /device:TPU:1, one launch (start us, length us, event | category | flops | bytes accessed | tf_op | source)
XLA Modules:
  0.0 53.6 jit_solution(7581203937403830103)
XLA Ops:
  0.0 52.1 %shard_map.64 = f32[32,512]{1,0:T(8,128)} custom-call(bf16[32,4,8192]{2,1,0:T(4,128)(2,1)} %traces_hbm.1, s32[1,32]{1,0:T(1,128)} %bitcast.4, s32[2,128]{1,0:T(2,128)} %bitcast.3, s32[1,32]{1,0:T(1,128)} %bitcast.5, bf16[32,256,256]{2,1,0:T(8,128)(2,1)} %constant.4.clone.table_hbm, bf16[32,256,512]{2,1,0:T(8,128)(2,1)} %constant.5.clone.lag_hbm), custom_call_target="tpu_custom_call" | custom-call | tf_op jit(solution)/shard_map/pallas_call | solution.py:413
  52.1 1.5 %copy.8 = f32[32,512]{1,0:T(8,128)} copy(f32[32,512]{1,0:T(8,128)} %shard_map.64) | data formatting | bytes 131072

commit v5 on v4

--- a/solution.py
+++ b/solution.py
@@ -18,9 +18,9 @@
 CH = 32
 SEG = 4
 EPS = 1e-06
-AHEAD = 3
-DELAY = 2
-PICKS = 4
+AHEAD = 4
+DELAY = 4
+PICKS = 8
 MESH = pl.DeviceIdType.MESH
 
 
@@ -81,9 +81,9 @@
 def kernel(
     rows, traces_hbm, alive_hbm, pair_hbm, window_hbm, table_hbm, lag_hbm, out_ref,
     alive_ref, pair_ref, window_ref, x, mid, spec, level, table, w,
-    both, lag, idx, first_pick, second_pick, total, piece, got,
+    both, lag, idx, first_pick, second_pick, total, piece, got, row_got, row_sum, late_sum,
     y_send, y_recv, own_send, own_recv, x_send, x_recv, rest_send, rest_recv,
-    idx_send, idx_recv, sum_send, sum_recv, local,
+    idx_send, idx_recv, sum_send, sum_recv, row_send, row_recv, late_send, late_recv, local,
 ):
     me, seg = lax.axis_index("chan"), lax.axis_index("seg")
     row, y = me // ROW, me % ROW
@@ -124,12 +124,17 @@
     fetch_lag.start()
 
     greet(sibling)
-    for k in range(8):
+    for k in range(1, 8):
         for c in range(2):
-            if k:
-                greet(at(row, (mine + k) % 8, c))
-            greet(at(before, (mine + k) % 8, c))
-            greet(at(after, (mine + k) % 8, c))
+            greet(at(row, (mine + k) % 8, c))
+    for r in (before, after):
+        for c in range(2):
+            greet((r * ROW + y, zh * 2 + c))
+
+        @pl.when(core == 1)
+        def _(r=r):
+            for k in range(1, ROW):
+                greet((r * ROW + (y + k) % ROW, seg))
 
     def column(values):
         n = values.shape[1]
@@ -170,7 +175,7 @@
             level[...] += jnp.sqrt(re * re + im * im)
             return carry
 
-        lax.fori_loop(0, UNITS, second_stage, 0, unroll=4)
+        lax.fori_loop(0, UNITS, second_stage, 0, unroll=8)
         sums = level[...]
         level[...] = 1.0 / ((sums + pltpu.roll(sums, 64, 1)) * (1.0 / BAND) + EPS)
         scales = [level[pl.ds(s, 16, stride=SEG), :] * live[16 * h : 16 * h + 16] for s in range(SEG)]
@@ -212,7 +217,7 @@
         )
 
     def x_copy(h, u, side):
-        to = before if side == 0 else after
+        to = (row + rows - 1 + 2 * side) % rows
         return remote(
             w.at[h, y, 4 * side + u], both.at[1, h, u, my_segs, 0], x_send.at[side, h, u], x_recv.at[core, h, u],
             (to * ROW + y, zh * 2 + side),
@@ -223,21 +228,23 @@
             w.at[h, y, u], both.at[1, h, u, pl.ds(SEG * c, SEG), 0], x_send.at[0, h, u], x_recv.at[c, h, u], sibling
         )
 
-    def rest_copy(h, u):
+    def rest_copy(d, h, u):
         to = (row + rows - 1 + 2 * core) % rows
-        others = pl.ds(1, 3)
         return remote(
-            both.at[0, h, u, :, others], both.at[1, h, u, :, others], rest_send.at[h, u], rest_recv.at[h, u],
+            both.at[0, h, u, :, d], both.at[1, h, u, :, d], rest_send.at[d - 1, h, u], rest_recv.at[d - 1, h, u],
             (to * ROW + y, seg),
         )
 
+    def item(step):
+        first = ((step % 2 == 0) & (step >= 2)) | (step == 15)
+        number = jnp.where(first, jnp.where(step == 15, 7, step // 2 - 1), (step + 1) // 2)
+        return jnp.where(first, 0, 1), number // 4, number % 4
+
     def start_y(step):
-        h, u = step // 4, step % 4
+        side, h, u = item(step)
         for d in (2, 1, 3):
-            for side in range(2):
-                y_copy(d, h, u, side).start()
-        for side in range(2):
-            x_copy(h, u, side).start()
+            y_copy(d, h, u, side).start()
+        x_copy(h, u, side).start()
 
     def idx_copy(k, slot):
         r = (row + core) % rows
@@ -246,9 +253,9 @@
     own_idx = pltpu.make_async_copy(pair_ref, idx.at[y], local.at[6])
 
     whiten(0)
-    pl.semaphore_wait(barrier, 47)
+    pl.semaphore_wait(barrier, 19 + 6 * core)
     for step in range(AHEAD):
-        start_y(step)
+        start_y(jnp.int32(step))
     for k in range(1, ROW):
         idx_copy(k, y).start()
 
@@ -286,32 +293,40 @@
     def spectra(side, u, s):
         return [both[side, h, u, s].reshape(64, 256) for h in range(2)]
 
-    def correlate(u):
+    def correlate(u, pairs):
         cross_re = cross_im = None
         for s in range(2 * SEG):
             near = jnp.concatenate(spectra(core, u, s), axis=0)
             far = jnp.concatenate(spectra(1 - core, u, s), axis=0)
-            a = jnp.dot(first_pick[...], near, preferred_element_type=jnp.float32)
-            b = jnp.dot(second_pick[...], jnp.concatenate([near, far], axis=0), preferred_element_type=jnp.float32)
+            a = jnp.dot(first_pick[pairs], near, preferred_element_type=jnp.float32)
+            b = jnp.dot(
+                second_pick[pairs], jnp.concatenate([near, far], axis=0), preferred_element_type=jnp.float32
+            )
             ar, ai, br, bi = a[:, :128], a[:, 128:], b[:, :128], b[:, 128:]
             re, im = ar * br + ai * bi, ai * br - ar * bi
             cross_re = re if cross_re is None else cross_re + re
             cross_im = im if cross_im is None else cross_im + im
         cross = jnp.concatenate([cross_re, cross_im], axis=1).astype(jnp.bfloat16)
-        total[...] += jnp.dot(cross, lag[u], preferred_element_type=jnp.float32)
+        total[pairs] += jnp.dot(cross, lag[u], preferred_element_type=jnp.float32)
 
     def advance(step, carry):
-        @pl.when(step + AHEAD < 8)
+        side, h, u = item(step)
+
+        @pl.when(step < 16)
+        def _():
+            for d in (1, 3, 2):
+                y_copy(d, h, u, side).wait_send()
+
+        @pl.when(step + AHEAD < 16)
         def _():
             start_y(step + AHEAD)
 
-        @pl.when(step < 8)
+        @pl.when((step < 16) & (side == core))
         def _():
-            h, u = step // 4, step % 4
             for d in (1, 3, 2):
                 for c in range(2):
                     y_arrival(d, h, u, c).wait_recv()
-            rest_copy(h, u).start()
+                rest_copy(d, h, u).start()
 
         @pl.when(step == PICKS)
         def _():
@@ -331,49 +346,87 @@
                 keep_own(h).wait()
                 take_own(h).wait_recv()
 
-        @pl.when(step >= 4 + DELAY)
+        side, h, u = item(jnp.maximum(step - DELAY, 0))
+
+        @pl.when((side == core) & (h == 1) & (u < 3))
         def _():
-            u = (step - DELAY) % 4
-            for h in range(2):
-                for c in range(2):
-                    x_arrival(h, u, c).wait_recv()
-                rest_copy(h, u).wait_recv()
-            correlate(u)
+            x_wait(u)
+            correlate(u, pl.ds(0, 512))
 
         return carry
 
-    lax.fori_loop(0, 8 + DELAY, advance, 0)
-
-    def sum_copy(k, c):
-        q = (mine + k) % 8
-        return remote(piece.at[q, c], got.at[core, k], sum_send.at[k, c], sum_recv.at[core, k], at(pair_row, q, c))
-
-    def sum_arrival(side, k):
-        return remote(piece.at[0, 0], got.at[side, k], sum_send.at[k, 0], sum_recv.at[side, k], sibling)
-
-    for k in (4, 5, 3, 7, 1, 6, 2, 0):
-        q = (mine + k) % 8
+    def x_wait(u):
+        for h in range(2):
+            for c in range(2):
+                x_arrival(h, u, c).wait_recv()
+            for d in (1, 3, 2):
+                rest_copy(d, h, u).wait_recv()
+
+    lax.fori_loop(0, 15 + DELAY, advance, 0)
+
+    def sum_copy(q, c):
+        return remote(piece.at[q, c], got.at[mine], sum_send.at[q, c], sum_recv.at[mine], at(row, q, c))
+
+    def sum_arrival(q):
+        return remote(piece.at[0, 0], got.at[q], sum_send.at[0, 0], sum_recv.at[q], sibling)
+
+    def row_copy(q):
+        return remote(piece.at[q], row_got.at[mine], row_send.at[q], row_recv.at[mine], at(row, q, 1))
+
+    def row_arrival(q):
+        return remote(piece.at[q], row_got.at[q], row_send.at[q], row_recv.at[q], sibling)
+
+    def late_copy(c):
+        return remote(row_sum.at[c], late_sum, late_send.at[c], late_recv, (before * ROW + y, zh * 2 + c))
+
+    x_wait(3)
+
+    def finish(i, carry):
+        half = (y // 2 + 1 + i) % 2
+        correlate(3, pl.ds(pl.multiple_of(half * 256, 256), 256))
+
+        for k in range(4):
+            q = half * 4 + (mine + k) % 4
+            for c in range(2):
+                piece[q, c] = total[pl.ds(pl.multiple_of(q * 64 + c * 32, 32), 32), :].astype(jnp.bfloat16)
+
+            @pl.when(core == 0)
+            def _(q=q):
+                @pl.when(q != mine)
+                def _():
+                    sum_copy(q, 0).start()
+
+                sum_copy(q, 1).start()
+
+            @pl.when((core == 1) & (q != mine))
+            def _(q=q):
+                row_copy(q).start()
+
+        return carry
+
+    lax.fori_loop(0, 2, finish, 0)
+
+    @pl.when(core == 0)
+    def _():
+        got[mine] = piece[mine, 0]
+
+    @pl.when(core == 1)
+    def _():
+        for k in range(1, 8):
+            row_arrival((mine + k) % 8).wait_recv()
         for c in range(2):
-            piece[q, c] = total[pl.ds(pl.multiple_of(q * 64 + c * 32, 32), 32), :].astype(jnp.bfloat16)
-            if k or c:
-                sum_copy(k, c).start()
-    stays = core == 0
-
-    @pl.when(stays)
-    def _():
-        got[0, 0] = piece[mine, 0]
-
-    @pl.when(core == 1)
-    def _():
-        sum_copy(0, 0).start()
+            sums = total[pl.ds(pl.multiple_of(mine * 64 + c * 32, 32), 32), :]
+            for k in range(1, 8):
+                sums = sums + row_got[(mine + k) % 8, c].astype(jnp.float32)
+            row_sum[c] = sums.astype(jnp.bfloat16)
+            late_copy(c).start()
 
     def sent(u, carry):
         for h in range(2):
             for side in range(2):
-                for d in (1, 2, 3):
-                    y_copy(d, h, u, side).wait_send()
                 x_copy(h, u, side).wait_send()
-            rest_copy(h, u).wait_send()
+            for d in (1, 2, 3):
+                rest_copy(d, h, u).wait_send()
         return carry
 
     lax.fori_loop(0, 4, sent, 0)
@@ -385,25 +438,31 @@
     @pl.when(core == 1)
     def _():
         idx_copy(0, y).wait_send()
-        sum_arrival(0, 0).wait_recv()
+        sum_arrival(mine).wait_recv()
 
     widest = column(window_ref[...])
     lags = jnp.abs(lax.broadcasted_iota(jnp.int32, (32, LAGS), 1) - LAGS // 2).astype(jnp.float32)
-    for side, k in [(0, k) for k in range(1, 8)] + [(1, k) for k in range(8)]:
-        sum_arrival(side, k).wait_recv()
-    result = jnp.zeros((32, LAGS), jnp.float32)
-    for side in range(2):
+    late_copy(0).wait_recv()
+    result = late_sum[...].astype(jnp.float32)
+    for k in range(1, 8):
+        sum_arrival((mine + k) % 8).wait_recv()
+    for k in range(8):
+        result = result + got[k].astype(jnp.float32)
+    out_ref[...] = jnp.where(lags <= widest, result, 0.0)
+    @pl.when(core == 0)
+    def _():
         for k in range(8):
-            result = result + got[side, k].astype(jnp.float32)
-    out_ref[...] = jnp.where(lags <= widest, result, 0.0)
-    for k in range(8):
+            q = (mine + k) % 8
+            if k:
+                sum_copy(q, 0).wait_send()
+            sum_copy(q, 1).wait_send()
+
+    @pl.when(core == 1)
+    def _():
+        for k in range(1, 8):
+            row_copy((mine + k) % 8).wait_send()
         for c in range(2):
-            if k or c:
-                sum_copy(k, c).wait_send()
-
-    @pl.when(core == 1)
-    def _():
-        sum_copy(0, 0).wait_send()
+            late_copy(c).wait_send()
 
 
 def body(traces, alive, pair_chan, lag_window):
@@ -432,19 +491,26 @@
             pltpu.VMEM((512, 256), jnp.bfloat16),
             pltpu.VMEM((512, LAGS), jnp.float32),
             pltpu.VMEM((8, 2, 32, LAGS), jnp.bfloat16),
-            pltpu.VMEM((2, 8, 32, LAGS), jnp.bfloat16),
+            pltpu.VMEM((8, 32, LAGS), jnp.bfloat16),
+            pltpu.VMEM((8, 2, 32, LAGS), jnp.bfloat16),
+            pltpu.VMEM((2, 32, LAGS), jnp.bfloat16),
+            pltpu.VMEM((32, LAGS), jnp.bfloat16),
             dma((2, 3, 2, 4)),
             dma((2, 3, 2, 4)),
             dma((2,)),
             dma((2,)),
             dma((2, 2, 4)),
             dma((2, 2, 4)),
-            dma((2, 4)),
-            dma((2, 4)),
+            dma((3, 2, 4)),
+            dma((3, 2, 4)),
             dma((ROW,)),
             dma((ROW,)),
             dma((8, 2)),
-            dma((2, 8)),
+            dma((8,)),
+            dma((8,)),
+            dma((8,)),
+            dma((2,)),
+            dma,
             dma((10,)),
         ],
         compiler_params=pltpu.CompilerParams(

time: 53.8 us -> 52.6 us (0.978)
  Pallas kernels: 52.1 us -> 50.9 us
    pallas_call x1, Pallas kernels: 52.1 us -> 50.9 us  [body(): pl.pallas_call(functools.partial(kernel, rows), out_shape=jax.ShapeDtypeS...]
where the time goes in v5:
time: 52.6 us; the launch traced here: 52.4 us
  Pallas kernels  50.9 us (97%)
  local copies, waits for them, and re-layouts  1.47 us (3%)
    pallas_call x1, Pallas kernels, body(): pl.pallas_call(functools.partial(kernel, rows), out_shape=jax.ShapeDtypeS...  50.9 us
    unnamed x1, local copies, waits for them, and re-layouts  1.47 us

profile of v5, /device:TPU:1, one launch (start us, length us, event | category | flops | bytes accessed | tf_op | source)
XLA Modules:
  0.0 52.4 jit_solution(6233695118981701905)
XLA Ops:
  0.0 50.9 %shard_map.64 = f32[32,512]{1,0:T(8,128)} custom-call(bf16[32,4,8192]{2,1,0:T(4,128)(2,1)} %traces_hbm.1, s32[1,32]{1,0:T(1,128)} %bitcast.4, s32[2,128]{1,0:T(2,128)} %bitcast.3, s32[1,32]{1,0:T(1,128)} %bitcast.5, bf16[32,256,256]{2,1,0:T(8,128)(2,1)} %constant.4.clone.table_hbm, bf16[32,256,512]{2,1,0:T(8,128)(2,1)} %constant.5.clone.lag_hbm), custom_call_target="tpu_custom_call" | custom-call | tf_op jit(solution)/shard_map/pallas_call | solution.py:472
  50.9 1.5 %copy.8 = f32[32,512]{1,0:T(8,128)} copy(f32[32,512]{1,0:T(8,128)} %shard_map.64) | data formatting | bytes 131072

commit v6 on v5

--- a/solution.py
+++ b/solution.py
@@ -272,7 +272,6 @@
     whiten(1)
     give_own(1).start()
     keep_own(1).start()
-    total[...] = jnp.zeros_like(total)
 
     channel_row = lax.broadcasted_iota(jnp.int32, (128, 128), 0)
     source_y = (y + ROW - (channel_row // 16) % ROW) % ROW
@@ -350,6 +349,10 @@
 
         @pl.when((side == core) & (h == 1) & (u < 3))
         def _():
+            @pl.when(u == 0)
+            def _():
+                total[...] = jnp.zeros_like(total)
+
             x_wait(u)
             correlate(u, pl.ds(0, 512))
 

time: 52.6 us -> 53.2 us (1.011)
  Pallas kernels: 50.9 us -> 51.6 us
    pallas_call x1, Pallas kernels: 50.9 us -> 51.6 us  [body(): pl.pallas_call(functools.partial(kernel, rows), out_shape=jax.ShapeDtypeS...]
where the time goes in v6:
time: 53.2 us; the launch traced here: 53 us
  Pallas kernels  51.6 us (97%)
  local copies, waits for them, and re-layouts  1.47 us (3%)
    pallas_call x1, Pallas kernels, body(): pl.pallas_call(functools.partial(kernel, rows), out_shape=jax.ShapeDtypeS...  51.6 us
    unnamed x1, local copies, waits for them, and re-layouts  1.47 us

profile of v6, /device:TPU:1, one launch (start us, length us, event | category | flops | bytes accessed | tf_op | source)
XLA Modules:
  0.0 53.0 jit_solution(2502151127470029058)
XLA Ops:
  0.0 51.6 %shard_map.64 = f32[32,512]{1,0:T(8,128)} custom-call(bf16[32,4,8192]{2,1,0:T(4,128)(2,1)} %traces_hbm.1, s32[1,32]{1,0:T(1,128)} %bitcast.4, s32[2,128]{1,0:T(2,128)} %bitcast.3, s32[1,32]{1,0:T(1,128)} %bitcast.5, bf16[32,256,256]{2,1,0:T(8,128)(2,1)} %constant.4.clone.table_hbm, bf16[32,256,512]{2,1,0:T(8,128)(2,1)} %constant.5.clone.lag_hbm), custom_call_target="tpu_custom_call" | custom-call | tf_op jit(solution)/shard_map/pallas_call | solution.py:475
  51.6 1.5 %copy.8 = f32[32,512]{1,0:T(8,128)} copy(f32[32,512]{1,0:T(8,128)} %shard_map.64) | data formatting | bytes 131072

commit v7 on v5

--- a/solution.py
+++ b/solution.py
@@ -442,12 +442,13 @@
 
     widest = column(window_ref[...])
     lags = jnp.abs(lax.broadcasted_iota(jnp.int32, (32, LAGS), 1) - LAGS // 2).astype(jnp.float32)
+    result = got[mine].astype(jnp.float32)
+    for k in range(1, 8):
+        q = (mine + k) % 8
+        sum_arrival(q).wait_recv()
+        result = result + got[q].astype(jnp.float32)
     late_copy(0).wait_recv()
-    result = late_sum[...].astype(jnp.float32)
-    for k in range(1, 8):
-        sum_arrival((mine + k) % 8).wait_recv()
-    for k in range(8):
-        result = result + got[k].astype(jnp.float32)
+    result = result + late_sum[...].astype(jnp.float32)
     out_ref[...] = jnp.where(lags <= widest, result, 0.0)
     @pl.when(core == 0)
     def _():

time: 52.6 us -> 52.6 us (level)
  no operation moved by 1% of the time
where the time goes in v7:
time: 52.6 us; the launch traced here: 52.4 us
  Pallas kernels  50.9 us (97%)
  local copies, waits for them, and re-layouts  1.47 us (3%)
    pallas_call x1, Pallas kernels, body(): pl.pallas_call(functools.partial(kernel, rows), out_shape=jax.ShapeDtypeS...  50.9 us
    unnamed x1, local copies, waits for them, and re-layouts  1.47 us

profile of v7, /device:TPU:1, one launch (start us, length us, event | category | flops | bytes accessed | tf_op | source)
XLA Modules:
  0.0 52.4 jit_solution(2770067526112721845)
XLA Ops:
  0.0 50.9 %shard_map.64 = f32[32,512]{1,0:T(8,128)} custom-call(bf16[32,4,8192]{2,1,0:T(4,128)(2,1)} %traces_hbm.1, s32[1,32]{1,0:T(1,128)} %bitcast.4, s32[2,128]{1,0:T(2,128)} %bitcast.3, s32[1,32]{1,0:T(1,128)} %bitcast.5, bf16[32,256,256]{2,1,0:T(8,128)(2,1)} %constant.4.clone.table_hbm, bf16[32,256,512]{2,1,0:T(8,128)(2,1)} %constant.5.clone.lag_hbm), custom_call_target="tpu_custom_call" | custom-call | tf_op jit(solution)/shard_map/pallas_call | solution.py:473
  50.9 1.5 %copy.8 = f32[32,512]{1,0:T(8,128)} copy(f32[32,512]{1,0:T(8,128)} %shard_map.64) | data formatting | bytes 131072
